TPU v7x, 256 devices: a whole 4x4x8 slice. The times are simulated.
256 devices in a mesh: seq: 32 (over x, z_hi, core), head: 8 (over z_lo, y).
Axes of the slice: x: 4, y: 4, z: 8 (z_hi: 4, z_lo: 2; z = z_hi * 2 + z_lo), core: 2. Of those that a mesh axis runs over, the one named last changes fastest.
Arguments:
- queries: bfloat16 [4096, 24576], P('seq', 'head'), may hold values from -200 to 200
- latent_keys: bfloat16 [4096, 576], P('seq'), may hold values from -8 to 8
- w_key_up: bfloat16 [128, 128, 512], P('head'), may hold values from -0.5 to 0.5
- w_value_up: bfloat16 [128, 512, 128], P('head'), may hold values from -0.25 to 0.25
- slab_order: int32 [32], replicated, may hold values from 0 to 31, each once
- segment_ids: int32 [4096], replicated, may hold values from 0 to 1, as said below
Outputs:
- attended: bfloat16 [4096, 16384], P(('seq', 'head'))
Inputs may be any that keep to these rules, and one draw needn't show every extreme that they name: `slab_order`: a permutation of the slab indices. `segment_ids`: never falls along positions; starts at 0, ends at 1, and each of the two transcripts holds 1024 positions or more.
All inputs are finite; a program needn't handle non-finite values.
Results may differ from a plain program's by a relative error of at most 0.0075.
Values may be sent and summed in bfloat16 or wider, within the bound.
A program may use at most 64 MiB of HBM per device.

v0:
```python
import jax
import jax.numpy as jnp
from jax import lax
from jax.sharding import PartitionSpec as P

negative_fill = -1e30


def right_product(left, block):
    return lax.dot_general(
        left, block, (((1,), (1,)), ((), ())), preferred_element_type=jnp.float32
    )


def shards(queries, latent_keys, w_key_up, w_value_up, slab_order, segment_ids):
    slab_rows = queries.shape[0]
    heads_here, nope_width, latent_width = w_key_up.shape
    rope_width = latent_keys.shape[1] - latent_width
    value_width = w_value_up.shape[2]
    scale = (nope_width + rope_width) ** (-0.5)
    query_rows = heads_here * slab_rows
    shaped = queries.reshape(slab_rows, heads_here, nope_width + rope_width)
    absorbed = jnp.einsum(
        "thn,hnc->htc", shaped[:, :, :nope_width], w_key_up, preferred_element_type=jnp.float32
    )
    absorbed = absorbed.astype(jnp.bfloat16).reshape(query_rows, latent_width)
    query_rope = shaped[:, :, nope_width:].transpose(1, 0, 2).reshape(query_rows, rope_width)
    my_slab = slab_order[lax.axis_index("seq")]
    query_pos = my_slab * slab_rows + jnp.arange(slab_rows, dtype=jnp.int32)
    query_seg = lax.dynamic_slice_in_dim(segment_ids, my_slab * slab_rows, slab_rows)
    slab_ids = jnp.arange(slab_order.shape[0], dtype=jnp.int32)

    def key_block(carry, block, first_row):
        width = block.shape[0]
        stored = first_row + jnp.arange(width, dtype=jnp.int32)
        owner = stored // slab_rows
        slab = jnp.sum(
            jnp.where(owner[:, None] == slab_ids[None, :], slab_order[None, :], 0), axis=1
        )
        key_pos = slab * slab_rows + stored % slab_rows
        key_seg = jnp.take(segment_ids, key_pos)
        live = (key_pos[None, :] <= query_pos[:, None]) & (key_seg[None, :] == query_seg[:, None])

        def update(state):
            running_top, running_total, running_acc = state
            scores = right_product(absorbed, block[:, :latent_width]) + right_product(
                query_rope, block[:, latent_width:]
            )
            scores = scores.reshape(heads_here, slab_rows, width) * scale
            mask = live[None, :, :]
            masked = jnp.where(mask, scores, negative_fill)
            new_top = jnp.maximum(running_top, jnp.max(masked, axis=2).reshape(query_rows))
            weights = jnp.where(
                mask, jnp.exp(masked - new_top.reshape(heads_here, slab_rows, 1)), 0.0
            )
            weights = weights.reshape(query_rows, width)
            fade = jnp.exp(running_top - new_top)
            new_total = running_total * fade + jnp.sum(weights, axis=1)
            new_acc = running_acc * fade[:, None] + jnp.dot(
                weights.astype(jnp.bfloat16),
                block[:, :latent_width],
                preferred_element_type=jnp.float32,
            )
            return (new_top, new_total, new_acc)

        return lax.cond(jnp.any(live), update, lambda state: state, carry)

    initial = (
        jnp.full((query_rows,), negative_fill, jnp.float32),
        jnp.zeros((query_rows,), jnp.float32),
        jnp.zeros((query_rows, latent_width), jnp.float32),
    )
    piece = lax.all_gather(latent_keys, "seq", axis=0, tiled=True)
    piece_rows = piece.shape[0]
    block_rows = 512

    def advance(step, state):
        block = lax.dynamic_slice_in_dim(piece, step * block_rows, block_rows)
        return key_block(state, block, step * block_rows)

    final_top, final_total, final_acc = lax.fori_loop(0, piece_rows // block_rows, advance, initial)
    context = (
        (final_acc / final_total[:, None])
        .astype(jnp.bfloat16)
        .reshape(heads_here, slab_rows, latent_width)
    )
    values = jnp.einsum("htc,hcv->thv", context, w_value_up, preferred_element_type=jnp.float32)
    values = values.astype(jnp.bfloat16).reshape(slab_rows, heads_here * value_width)
    return lax.all_to_all(values, "head", split_axis=0, concat_axis=1, tiled=True)


def solution(mesh):
    in_specs = (
        P("seq", "head"),
        P("seq", None),
        P("head", None, None),
        P("head", None, None),
        P(),
        P(),
    )
    out_specs = P(("seq", "head"), None)
    return jax.shard_map(shards, mesh=mesh, in_specs=in_specs, out_specs=out_specs, check_vma=False)
```

profile of v0, /device:TPU:195, one launch (start us, length us, event | category | flops | bytes accessed | tf_op | source)
XLA Modules:
  0.0 245.2 jit_solution(5470909100071839738)
XLA Ops:
  14.6 2.1 convolution_convert_fusion
  16.6 57.1 %all-gather.2.cloned.1.call-done = bf16[4096,576]{1,0:T(8,128)(2,1)} async-done(((bf16[128,576]{1,0:T(8,128)(2,1)}), bf16[4096,576]{1,0:T(8,128)(2,1)}) %all-gather.2.cloned.1.call-update) | async-done | bytes 4718608 | tf_op jit(solution)/shard_map/all_gather | solution.py:73
  73.7 2.5 %broadcast_in_dim.95 = f32[2048,512]{1,0:T(8,128)} broadcast(f32[]{:T(128)} %constant.166.clone.1), dimensions={} | broadcast | bytes 4194308 | tf_op jit(solution)/shard_map/broadcast_in_dim | solution.py:71
  76.3 145.8 %while.20 = (s32[]{:T(128)}, f32[2048]{0:T(1024)S(1)}, f32[2048]{0:T(1024)S(1)}, f32[2048,512]{1,0:T(8,128)}, s32[32]{0:T(128)S(1)}, /*index=5*/s32[4096]{0:T(10...) while((s32[]{:T(128)}, f32[2048]{0:T(1024)S(1)}, ...), condition=%wide.region_7.8_spmd.clone, body=%wide.region_0.7_spmd.clone.sunk | while | flops 2294628096 | bytes 70950928 | solution.py:81
  76.4 3.1 %gather_fusion = s32[512]{0:T(512)S(1)} fusion(s32[4096]{0:T(1024)S(1)} %get-tuple-element.578, s32[1024]{0:T(1024)S(1)} %pad_clamp_fusion.2), kind=kCustom, calls=%fused_computation.clone.clone.1 | custom fusion | bytes 6144 | tf_op jit(solution)/shard_map/while/body/eval_jaxpr/jit(_take)/gather | solution.py:41
  81.2 13.3 %conditional.3 = ((f32[2048]{0:T(1024)S(1)}, f32[2048]{0:T(1024)S(1)}, f32[2048,512]{1,0:T(8,128)})) conditional(s32[]{:T(128)} %convert_element_type.39, (f32[2048]{0:T(1024)S(1)}, f32[2048]{0:T(1024)S(1)}, f32[2048,512]{1,0:T(8,128)}) %tuple.64, (pred[128,512]{0,1:T(8,128)(4,1)S(1)}, s32[]{:T(128)}, bf16[4096,576]{1,0:T(8,128)(2,1)}, ...), branch_computations={%region_3.3_spmd, %region_4.6_spmd} | conditional | flops 2294288384 | bytes 70844568 | solution.py:66
  81.5 3.1 %fusion.10 = f32[512,2048]{1,0:T(8,128)S(1)} fusion(bf16[2048,512]{1,0:T(8,128)(2,1)} %get-tuple-element.355, bf16[4096,576]{1,0:T(8,128)(2,1)} %get-tuple-element.353, s32[]{:T(128)S(6)} %select_n.137), kind=kOutput, calls=%fused_computation.11 | convolution fusion | flops 1073741824 | bytes 6815748 | tf_op jit(solution)/shard_map/while/body/eval_jaxpr/cond/branch_1_fun/dot_general | solution.py:10
  84.6 2.1 fusion.26
  88.9 3.6 %multiply_add_fusion = f32[2048,512]{1,0:T(8,128)S(1)} fusion(f32[2048,512]{1,0:T(8,128)S(1)} %copy-done.2, f32[2048,512]{0,1:T(8,128)S(1)} %get-tuple-element.459, pred[64,8,16,128]{3,2,1,0:T(8,128)(4,1)S(1)} %bitcast.38, f32[2048]{0:T(1024)S(1)} %get-tuple-element.453, f32[2048]{0:T(1024)S(1)} %max.3, bf16[4096,576]{1,0:T(8,128)(2,1)} %get-tuple-element.353, ...), kind=kOutput, calls=%fused_computation.4 | convolution fusion | flops 1078984704 | bytes 14172164 | tf_op jit(solution)/shard_map/while/body/eval_jaxpr/cond/branch_1_fun/dot_general | solution.py:59
  92.5 2.0 copy-done.3
  94.7 3.1 %gather_fusion = s32[512]{0:T(512)S(1)} fusion(s32[4096]{0:T(1024)S(1)} %get-tuple-element.578, s32[1024]{0:T(1024)S(1)} %pad_clamp_fusion.2), kind=kCustom, calls=%fused_computation.clone.clone.1 | custom fusion | bytes 6144 | tf_op jit(solution)/shard_map/while/body/eval_jaxpr/jit(_take)/gather | solution.py:41
  99.4 13.3 %conditional.3 = ((f32[2048]{0:T(1024)S(1)}, f32[2048]{0:T(1024)S(1)}, f32[2048,512]{1,0:T(8,128)})) conditional(s32[]{:T(128)} %convert_element_type.39, (f32[2048]{0:T(1024)S(1)}, f32[2048]{0:T(1024)S(1)}, f32[2048,512]{1,0:T(8,128)}) %tuple.64, (pred[128,512]{0,1:T(8,128)(4,1)S(1)}, s32[]{:T(128)}, bf16[4096,576]{1,0:T(8,128)(2,1)}, ...), branch_computations={%region_3.3_spmd, %region_4.6_spmd} | conditional | flops 2294288384 | bytes 70844568 | solution.py:66
  99.8 3.1 %fusion.10 = f32[512,2048]{1,0:T(8,128)S(1)} fusion(bf16[2048,512]{1,0:T(8,128)(2,1)} %get-tuple-element.355, bf16[4096,576]{1,0:T(8,128)(2,1)} %get-tuple-element.353, s32[]{:T(128)S(6)} %select_n.137), kind=kOutput, calls=%fused_computation.11 | convolution fusion | flops 1073741824 | bytes 6815748 | tf_op jit(solution)/shard_map/while/body/eval_jaxpr/cond/branch_1_fun/dot_general | solution.py:10
  102.8 2.1 fusion.26
  107.1 3.6 %multiply_add_fusion = f32[2048,512]{1,0:T(8,128)S(1)} fusion(f32[2048,512]{1,0:T(8,128)S(1)} %copy-done.2, f32[2048,512]{0,1:T(8,128)S(1)} %get-tuple-element.459, pred[64,8,16,128]{3,2,1,0:T(8,128)(4,1)S(1)} %bitcast.38, f32[2048]{0:T(1024)S(1)} %get-tuple-element.453, f32[2048]{0:T(1024)S(1)} %max.3, bf16[4096,576]{1,0:T(8,128)(2,1)} %get-tuple-element.353, ...), kind=kOutput, calls=%fused_computation.4 | convolution fusion | flops 1078984704 | bytes 14172164 | tf_op jit(solution)/shard_map/while/body/eval_jaxpr/cond/branch_1_fun/dot_general | solution.py:59
  112.9 3.1 %gather_fusion = s32[512]{0:T(512)S(1)} fusion(s32[4096]{0:T(1024)S(1)} %get-tuple-element.578, s32[1024]{0:T(1024)S(1)} %pad_clamp_fusion.2), kind=kCustom, calls=%fused_computation.clone.clone.1 | custom fusion | bytes 6144 | tf_op jit(solution)/shard_map/while/body/eval_jaxpr/jit(_take)/gather | solution.py:41
  117.7 13.3 %conditional.3 = ((f32[2048]{0:T(1024)S(1)}, f32[2048]{0:T(1024)S(1)}, f32[2048,512]{1,0:T(8,128)})) conditional(s32[]{:T(128)} %convert_element_type.39, (f32[2048]{0:T(1024)S(1)}, f32[2048]{0:T(1024)S(1)}, f32[2048,512]{1,0:T(8,128)}) %tuple.64, (pred[128,512]{0,1:T(8,128)(4,1)S(1)}, s32[]{:T(128)}, bf16[4096,576]{1,0:T(8,128)(2,1)}, ...), branch_computations={%region_3.3_spmd, %region_4.6_spmd} | conditional | flops 2294288384 | bytes 70844568 | solution.py:66
  118.0 3.1 %fusion.10 = f32[512,2048]{1,0:T(8,128)S(1)} fusion(bf16[2048,512]{1,0:T(8,128)(2,1)} %get-tuple-element.355, bf16[4096,576]{1,0:T(8,128)(2,1)} %get-tuple-element.353, s32[]{:T(128)S(6)} %select_n.137), kind=kOutput, calls=%fused_computation.11 | convolution fusion | flops 1073741824 | bytes 6815748 | tf_op jit(solution)/shard_map/while/body/eval_jaxpr/cond/branch_1_fun/dot_general | solution.py:10
  121.0 2.1 fusion.26
  125.4 3.6 %multiply_add_fusion = f32[2048,512]{1,0:T(8,128)S(1)} fusion(f32[2048,512]{1,0:T(8,128)S(1)} %copy-done.2, f32[2048,512]{0,1:T(8,128)S(1)} %get-tuple-element.459, pred[64,8,16,128]{3,2,1,0:T(8,128)(4,1)S(1)} %bitcast.38, f32[2048]{0:T(1024)S(1)} %get-tuple-element.453, f32[2048]{0:T(1024)S(1)} %max.3, bf16[4096,576]{1,0:T(8,128)(2,1)} %get-tuple-element.353, ...), kind=kOutput, calls=%fused_computation.4 | convolution fusion | flops 1078984704 | bytes 14172164 | tf_op jit(solution)/shard_map/while/body/eval_jaxpr/cond/branch_1_fun/dot_general | solution.py:59
  129.0 2.0 copy-done.3
  131.1 3.1 %gather_fusion = s32[512]{0:T(512)S(1)} fusion(s32[4096]{0:T(1024)S(1)} %get-tuple-element.578, s32[1024]{0:T(1024)S(1)} %pad_clamp_fusion.2), kind=kCustom, calls=%fused_computation.clone.clone.1 | custom fusion | bytes 6144 | tf_op jit(solution)/shard_map/while/body/eval_jaxpr/jit(_take)/gather | solution.py:41
  135.9 13.3 %conditional.3 = ((f32[2048]{0:T(1024)S(1)}, f32[2048]{0:T(1024)S(1)}, f32[2048,512]{1,0:T(8,128)})) conditional(s32[]{:T(128)} %convert_element_type.39, (f32[2048]{0:T(1024)S(1)}, f32[2048]{0:T(1024)S(1)}, f32[2048,512]{1,0:T(8,128)}) %tuple.64, (pred[128,512]{0,1:T(8,128)(4,1)S(1)}, s32[]{:T(128)}, bf16[4096,576]{1,0:T(8,128)(2,1)}, ...), branch_computations={%region_3.3_spmd, %region_4.6_spmd} | conditional | flops 2294288384 | bytes 70844568 | solution.py:66
  136.2 3.1 %fusion.10 = f32[512,2048]{1,0:T(8,128)S(1)} fusion(bf16[2048,512]{1,0:T(8,128)(2,1)} %get-tuple-element.355, bf16[4096,576]{1,0:T(8,128)(2,1)} %get-tuple-element.353, s32[]{:T(128)S(6)} %select_n.137), kind=kOutput, calls=%fused_computation.11 | convolution fusion | flops 1073741824 | bytes 6815748 | tf_op jit(solution)/shard_map/while/body/eval_jaxpr/cond/branch_1_fun/dot_general | solution.py:10
  139.3 2.1 fusion.26
  143.6 3.6 %multiply_add_fusion = f32[2048,512]{1,0:T(8,128)S(1)} fusion(f32[2048,512]{1,0:T(8,128)S(1)} %copy-done.2, f32[2048,512]{0,1:T(8,128)S(1)} %get-tuple-element.459, pred[64,8,16,128]{3,2,1,0:T(8,128)(4,1)S(1)} %bitcast.38, f32[2048]{0:T(1024)S(1)} %get-tuple-element.453, f32[2048]{0:T(1024)S(1)} %max.3, bf16[4096,576]{1,0:T(8,128)(2,1)} %get-tuple-element.353, ...), kind=kOutput, calls=%fused_computation.4 | convolution fusion | flops 1078984704 | bytes 14172164 | tf_op jit(solution)/shard_map/while/body/eval_jaxpr/cond/branch_1_fun/dot_general | solution.py:59
  149.3 3.1 %gather_fusion = s32[512]{0:T(512)S(1)} fusion(s32[4096]{0:T(1024)S(1)} %get-tuple-element.578, s32[1024]{0:T(1024)S(1)} %pad_clamp_fusion.2), kind=kCustom, calls=%fused_computation.clone.clone.1 | custom fusion | bytes 6144 | tf_op jit(solution)/shard_map/while/body/eval_jaxpr/jit(_take)/gather | solution.py:41
  154.1 13.3 %conditional.3 = ((f32[2048]{0:T(1024)S(1)}, f32[2048]{0:T(1024)S(1)}, f32[2048,512]{1,0:T(8,128)})) conditional(s32[]{:T(128)} %convert_element_type.39, (f32[2048]{0:T(1024)S(1)}, f32[2048]{0:T(1024)S(1)}, f32[2048,512]{1,0:T(8,128)}) %tuple.64, (pred[128,512]{0,1:T(8,128)(4,1)S(1)}, s32[]{:T(128)}, bf16[4096,576]{1,0:T(8,128)(2,1)}, ...), branch_computations={%region_3.3_spmd, %region_4.6_spmd} | conditional | flops 2294288384 | bytes 70844568 | solution.py:66
  154.4 3.1 %fusion.10 = f32[512,2048]{1,0:T(8,128)S(1)} fusion(bf16[2048,512]{1,0:T(8,128)(2,1)} %get-tuple-element.355, bf16[4096,576]{1,0:T(8,128)(2,1)} %get-tuple-element.353, s32[]{:T(128)S(6)} %select_n.137), kind=kOutput, calls=%fused_computation.11 | convolution fusion | flops 1073741824 | bytes 6815748 | tf_op jit(solution)/shard_map/while/body/eval_jaxpr/cond/branch_1_fun/dot_general | solution.py:10
  157.5 2.1 fusion.26
  161.8 3.6 %multiply_add_fusion = f32[2048,512]{1,0:T(8,128)S(1)} fusion(f32[2048,512]{1,0:T(8,128)S(1)} %copy-done.2, f32[2048,512]{0,1:T(8,128)S(1)} %get-tuple-element.459, pred[64,8,16,128]{3,2,1,0:T(8,128)(4,1)S(1)} %bitcast.38, f32[2048]{0:T(1024)S(1)} %get-tuple-element.453, f32[2048]{0:T(1024)S(1)} %max.3, bf16[4096,576]{1,0:T(8,128)(2,1)} %get-tuple-element.353, ...), kind=kOutput, calls=%fused_computation.4 | convolution fusion | flops 1078984704 | bytes 14172164 | tf_op jit(solution)/shard_map/while/body/eval_jaxpr/cond/branch_1_fun/dot_general | solution.py:59
  167.6 3.1 %gather_fusion = s32[512]{0:T(512)S(1)} fusion(s32[4096]{0:T(1024)S(1)} %get-tuple-element.578, s32[1024]{0:T(1024)S(1)} %pad_clamp_fusion.2), kind=kCustom, calls=%fused_computation.clone.clone.1 | custom fusion | bytes 6144 | tf_op jit(solution)/shard_map/while/body/eval_jaxpr/jit(_take)/gather | solution.py:41
  172.4 13.3 %conditional.3 = ((f32[2048]{0:T(1024)S(1)}, f32[2048]{0:T(1024)S(1)}, f32[2048,512]{1,0:T(8,128)})) conditional(s32[]{:T(128)} %convert_element_type.39, (f32[2048]{0:T(1024)S(1)}, f32[2048]{0:T(1024)S(1)}, f32[2048,512]{1,0:T(8,128)}) %tuple.64, (pred[128,512]{0,1:T(8,128)(4,1)S(1)}, s32[]{:T(128)}, bf16[4096,576]{1,0:T(8,128)(2,1)}, ...), branch_computations={%region_3.3_spmd, %region_4.6_spmd} | conditional | flops 2294288384 | bytes 70844568 | solution.py:66
  172.7 3.1 %fusion.10 = f32[512,2048]{1,0:T(8,128)S(1)} fusion(bf16[2048,512]{1,0:T(8,128)(2,1)} %get-tuple-element.355, bf16[4096,576]{1,0:T(8,128)(2,1)} %get-tuple-element.353, s32[]{:T(128)S(6)} %select_n.137), kind=kOutput, calls=%fused_computation.11 | convolution fusion | flops 1073741824 | bytes 6815748 | tf_op jit(solution)/shard_map/while/body/eval_jaxpr/cond/branch_1_fun/dot_general | solution.py:10
  175.7 2.1 fusion.26
  180.0 3.6 %multiply_add_fusion = f32[2048,512]{1,0:T(8,128)S(1)} fusion(f32[2048,512]{1,0:T(8,128)S(1)} %copy-done.2, f32[2048,512]{0,1:T(8,128)S(1)} %get-tuple-element.459, pred[64,8,16,128]{3,2,1,0:T(8,128)(4,1)S(1)} %bitcast.38, f32[2048]{0:T(1024)S(1)} %get-tuple-element.453, f32[2048]{0:T(1024)S(1)} %max.3, bf16[4096,576]{1,0:T(8,128)(2,1)} %get-tuple-element.353, ...), kind=kOutput, calls=%fused_computation.4 | convolution fusion | flops 1078984704 | bytes 14172164 | tf_op jit(solution)/shard_map/while/body/eval_jaxpr/cond/branch_1_fun/dot_general | solution.py:59
  185.8 3.1 %gather_fusion = s32[512]{0:T(512)S(1)} fusion(s32[4096]{0:T(1024)S(1)} %get-tuple-element.578, s32[1024]{0:T(1024)S(1)} %pad_clamp_fusion.2), kind=kCustom, calls=%fused_computation.clone.clone.1 | custom fusion | bytes 6144 | tf_op jit(solution)/shard_map/while/body/eval_jaxpr/jit(_take)/gather | solution.py:41
  190.6 13.3 %conditional.3 = ((f32[2048]{0:T(1024)S(1)}, f32[2048]{0:T(1024)S(1)}, f32[2048,512]{1,0:T(8,128)})) conditional(s32[]{:T(128)} %convert_element_type.39, (f32[2048]{0:T(1024)S(1)}, f32[2048]{0:T(1024)S(1)}, f32[2048,512]{1,0:T(8,128)}) %tuple.64, (pred[128,512]{0,1:T(8,128)(4,1)S(1)}, s32[]{:T(128)}, bf16[4096,576]{1,0:T(8,128)(2,1)}, ...), branch_computations={%region_3.3_spmd, %region_4.6_spmd} | conditional | flops 2294288384 | bytes 70844568 | solution.py:66
  190.9 3.1 %fusion.10 = f32[512,2048]{1,0:T(8,128)S(1)} fusion(bf16[2048,512]{1,0:T(8,128)(2,1)} %get-tuple-element.355, bf16[4096,576]{1,0:T(8,128)(2,1)} %get-tuple-element.353, s32[]{:T(128)S(6)} %select_n.137), kind=kOutput, calls=%fused_computation.11 | convolution fusion | flops 1073741824 | bytes 6815748 | tf_op jit(solution)/shard_map/while/body/eval_jaxpr/cond/branch_1_fun/dot_general | solution.py:10
  193.9 2.1 fusion.26
  198.3 3.6 %multiply_add_fusion = f32[2048,512]{1,0:T(8,128)S(1)} fusion(f32[2048,512]{1,0:T(8,128)S(1)} %copy-done.2, f32[2048,512]{0,1:T(8,128)S(1)} %get-tuple-element.459, pred[64,8,16,128]{3,2,1,0:T(8,128)(4,1)S(1)} %bitcast.38, f32[2048]{0:T(1024)S(1)} %get-tuple-element.453, f32[2048]{0:T(1024)S(1)} %max.3, bf16[4096,576]{1,0:T(8,128)(2,1)} %get-tuple-element.353, ...), kind=kOutput, calls=%fused_computation.4 | convolution fusion | flops 1078984704 | bytes 14172164 | tf_op jit(solution)/shard_map/while/body/eval_jaxpr/cond/branch_1_fun/dot_general | solution.py:59
  204.0 3.1 %gather_fusion = s32[512]{0:T(512)S(1)} fusion(s32[4096]{0:T(1024)S(1)} %get-tuple-element.578, s32[1024]{0:T(1024)S(1)} %pad_clamp_fusion.2), kind=kCustom, calls=%fused_computation.clone.clone.1 | custom fusion | bytes 6144 | tf_op jit(solution)/shard_map/while/body/eval_jaxpr/jit(_take)/gather | solution.py:41
  208.8 13.3 %conditional.3 = ((f32[2048]{0:T(1024)S(1)}, f32[2048]{0:T(1024)S(1)}, f32[2048,512]{1,0:T(8,128)})) conditional(s32[]{:T(128)} %convert_element_type.39, (f32[2048]{0:T(1024)S(1)}, f32[2048]{0:T(1024)S(1)}, f32[2048,512]{1,0:T(8,128)}) %tuple.64, (pred[128,512]{0,1:T(8,128)(4,1)S(1)}, s32[]{:T(128)}, bf16[4096,576]{1,0:T(8,128)(2,1)}, ...), branch_computations={%region_3.3_spmd, %region_4.6_spmd} | conditional | flops 2294288384 | bytes 70844568 | solution.py:66
  209.1 3.1 %fusion.10 = f32[512,2048]{1,0:T(8,128)S(1)} fusion(bf16[2048,512]{1,0:T(8,128)(2,1)} %get-tuple-element.355, bf16[4096,576]{1,0:T(8,128)(2,1)} %get-tuple-element.353, s32[]{:T(128)S(6)} %select_n.137), kind=kOutput, calls=%fused_computation.11 | convolution fusion | flops 1073741824 | bytes 6815748 | tf_op jit(solution)/shard_map/while/body/eval_jaxpr/cond/branch_1_fun/dot_general | solution.py:10
  212.2 2.1 fusion.26
  216.5 3.6 %multiply_add_fusion = f32[2048,512]{1,0:T(8,128)S(1)} fusion(f32[2048,512]{1,0:T(8,128)S(1)} %copy-done.2, f32[2048,512]{0,1:T(8,128)S(1)} %get-tuple-element.459, pred[64,8,16,128]{3,2,1,0:T(8,128)(4,1)S(1)} %bitcast.38, f32[2048]{0:T(1024)S(1)} %get-tuple-element.453, f32[2048]{0:T(1024)S(1)} %max.3, bf16[4096,576]{1,0:T(8,128)(2,1)} %get-tuple-element.353, ...), kind=kOutput, calls=%fused_computation.4 | convolution fusion | flops 1078984704 | bytes 14172164 | tf_op jit(solution)/shard_map/while/body/eval_jaxpr/cond/branch_1_fun/dot_general | solution.py:59
  222.1 2.7 %divide_convert_fusion = bf16[2048,512]{1,0:T(8,128)(2,1)S(1)} fusion(f32[2048,512]{1,0:T(8,128)} %get-tuple-element.377, f32[2048]{0:T(1024)S(1)} %get-tuple-element.378), kind=kLoop, calls=%fused_computation.44 | loop fusion | flops 2097152 | bytes 6299648 | tf_op jit(solution)/shard_map/convert_element_type | solution.py:84
  226.2 11.3 %all_to_all.19 = bf16[8,16,2048]{2,1,0:T(8,128)(2,1)S(1)} all-to-all(bf16[8,16,2048]{2,1,0:T(8,128)(2,1)S(1)} %all_to_all.14), channel_id=1, replica_groups=mesh['seq'=32,'head'=8] {'head'}, dimensions={0} | all-to-all | bytes 1048576 | tf_op jit(solution)/shard_map/all_to_all | solution.py:89
  (156 shorter events, 49.6 us)
Async XLA Ops:
  6.5 8.0 %copy-start = (bf16[16,128,512]{2,1,0:T(8,128)(2,1)S(1)}, bf16[16,128,512]{2,1,0:T(8,128)(2,1)}, u32[]{:S(2)}) copy-start(bf16[16,128,512]{2,1,0:T(8,128)(2,1)} %param.12) | copy-start | bytes 6291460
  6.5 67.2 %all-gather.2.cloned.1.call-start = ((), (), s32[]{:S(2)}) async-start(), calls=%async_computation.1 | async-start | bytes 5406720 | tf_op jit(solution)/shard_map/all_gather | solution.py:73
  14.6 61.7 %copy-start.1 = (s32[4096]{0:T(1024)S(1)}, s32[4096]{0:T(1024)}, u32[]{:S(2)}) copy-start(s32[4096]{0:T(1024)} %param.15) | copy-start | bytes 49156
  14.6 61.7 %copy-start.5 = (s32[32]{0:T(128)S(1)}, s32[32]{0:T(128)}, u32[]{:S(2)}) copy-start(s32[32]{0:T(128)} %param.14) | copy-start | bytes 388
  86.7 2.2 copy-start.2
  92.5 2.0 copy-start.3
  104.9 2.2 copy-start.2
  110.7 2.0 copy-start.3
  123.2 2.2 copy-start.2
  129.0 2.0 copy-start.3
  141.4 2.2 copy-start.2
  147.2 2.0 copy-start.3
  159.6 2.2 copy-start.2
  165.4 2.0 copy-start.3
  177.9 2.2 copy-start.2
  183.6 2.0 copy-start.3
  196.1 2.2 copy-start.2
  201.9 2.0 copy-start.3
  214.3 2.2 copy-start.2
  220.1 2.0 copy-start.3
  222.1 2.9 %copy-start.4 = (bf16[16,512,128]{2,1,0:T(8,128)(2,1)S(1)}, bf16[16,512,128]{2,1,0:T(8,128)(2,1)}, u32[]{:S(2)}) copy-start(bf16[16,512,128]{2,1,0:T(8,128)(2,1)} %param.13) | copy-start | bytes 6291460
Sparse Core Ops, SparseCore 0:
  9.9 63.7 all-gather.1
where the time goes:
time: 247 us; the launch traced here: 245 us
  matrix products  73 us (30%)
  local copies, waits for them, and re-layouts  63 us (26%)
  waiting for transfers between devices  57.1 us (23%)
  other arithmetic  20.3 us (8%)
  between operations  14.1 us (6%)
  blocking collectives  11.3 us (5%)
  loops' own time  6.48 us (3%)
    all_gather x1, waiting for transfers between devices, shards(): piece = lax.all_gather(latent_keys, 'seq', axis=0, tiled=True)  57.1 us
    dot_general x16, matrix products, right_product(): lax.dot_general(left, block, (((1,), (1,)), ((), ())), preferred_element_...  41.4 us
    dot_general x8, matrix products, update(): jnp.dot(weights.astype(jnp.bfloat16), block[:, :latent_width], preferred_...  28.8 us
    gather x8, local copies, waits for them, and re-layouts, key_block(): key_seg = jnp.take(segment_ids, key_pos)  25.1 us
    cond x40, local copies, waits for them, and re-layouts  24.2 us
    all_to_all x1, blocking collectives, shards(): lax.all_to_all(values, 'head', split_axis=0, concat_axis=1, tiled=True)  11.3 us
    reduce_sum x8, other arithmetic, update(): new_total = running_total * fade + jnp.sum(weights, axis=1)  8.9 us
    reduce_or x8, other arithmetic, key_block(): return lax.cond(jnp.any(live), update, lambda state: state, carry)  7.34 us
  transfers between devices with their start and end apart: 1, of which 1 were waited for; matrix products, arithmetic and copies ran while one was open for 3% of the time, Pallas kernels for 0%

commit v1 on v0

v1 whole, which is shorter than its diff:
```python
import functools

import jax
import jax.numpy as jnp
from jax import lax
from jax.experimental import pallas as pl
from jax.experimental.pallas import tpu as pltpu
from jax.sharding import PartitionSpec as P

MESH = pl.DeviceIdType.MESH
BF16 = jnp.bfloat16
F32 = jnp.float32

HEADS = 16
ROWS = 128
NOPE, ROPE, LATENT, VHEAD = 128, 64, 512, 128
KEY = LATENT + ROPE
WIDE = KEY + ROWS
SLABS = 32
WINDOW = 24
PAIR = 2 * ROWS
STEPS = HEADS // 2
CHUNK = 512
NEGATIVE = -1.0e30
LOG2E = 1.4426950408889634


def dot(a, b):
    return jnp.dot(a, b, preferred_element_type=F32)


def kernel(
    order, segment, latent, queries_hbm, w_key_hbm, w_value_hbm, out,
    gathered, wide_q, key_t, value, scores, tops, attended, queries, w_key, w_value,
    listed, load_sem, send_sem, recv_sem, half_sem, out_send, out_recv,
):
    seq, head = lax.axis_index("seq"), lax.axis_index("head")
    core, zh, x = seq % 2, (seq // 2) % 4, seq // 8
    y, zl = head % 4, head // 4

    def slab(x_of, zh_of, core_of):
        return (x_of * 4 + zh_of) * 2 + core_of

    x_up, x_down, x_far = (x + 1) % 4, (x + 3) % 4, (x + 2) % 4
    zh_outer = (zh + 3 + 2 * zl) % 4
    zh_inner = (zh + 5 - 2 * zl) % 4
    zh_far = (zh + 2) % 4
    up = (slab(x_up, zh, core), head)
    down = (slab(x_down, zh, core), head)
    outer = (slab(x, zh_outer, core), (1 - zl) * 4 + y)
    inner = (seq, (1 - zl) * 4 + y)
    twin = (slab(x, zh, 1 - core), head)
    mates = [(seq, (head + 1 + i) % 8) for i in range(7)]

    loads = [
        pltpu.make_async_copy(queries_hbm, queries, load_sem.at[0]),
        pltpu.make_async_copy(w_key_hbm, w_key, load_sem.at[1]),
        pltpu.make_async_copy(w_value_hbm, w_value, load_sem.at[2]),
    ]
    for load in loads:
        load.start()
    gathered[seq] = latent[...]

    barrier = pltpu.get_barrier_semaphore()
    greeted = [up, down, outer, twin] + mates
    for device in greeted:
        pl.semaphore_signal(barrier, inc=1, device_id=device, device_id_type=MESH)
    pl.semaphore_wait(barrier, len(greeted))

    def piece(index, half):
        if half is None:
            return gathered.at[index]
        return gathered.at[index, pl.ds(pl.multiple_of(half * 64, 64), 64)]

    def transfer(index, device, sent, half=None):
        arrived = recv_sem.at[index] if half is None else half_sem.at[half]
        return pltpu.make_async_remote_copy(
            src_ref=piece(index, half), dst_ref=piece(index, half),
            send_sem=send_sem.at[sent], recv_sem=arrived,
            device_id=device, device_id_type=MESH,
        )

    sent = ([], [])

    def send(which, index, device, half=None):
        transfer(index, device, len(sent[which]), half).start()
        sent[which].append(half)

    def arrive(index, half=None):
        transfer(index, twin, 0, half).wait_recv()

    @pl.when(core == 0)
    def _():
        for device in (up, down, twin, outer):
            send(0, seq, device)

    @pl.when(core == 1)
    def _():
        for device in (outer, twin, up, down):
            send(1, seq, device)

    def search(_, span):
        low, high = span
        middle = (low + high) // 2
        first = segment[middle] == 0
        return jnp.where(first, middle + 1, low), jnp.where(first, high, middle)

    boundary, _ = lax.fori_loop(0, 12, search, (0, SLABS * ROWS - 1))
    my_slab = order[seq]

    def invert(step, _):
        wanted = jnp.maximum(my_slab - step, 0)
        found = 0
        for b in range(1, SLABS):
            found = jnp.where(order[b] == wanted, b, found)
        listed[step] = found
        return 0

    lax.fori_loop(0, WINDOW, invert, 0)

    loads[0].wait()
    loads[1].wait()
    row = lax.broadcasted_iota(jnp.int32, (ROWS, ROWS), 0)
    column = lax.broadcasted_iota(jnp.int32, (ROWS, ROWS), 1)
    one_hot = (row == column).astype(BF16)

    def absorb(j, _):
        two = queries[:, pl.ds(pl.multiple_of(j * 384, 384), 384)]
        for i in range(2):
            mine = two[:, i * 192 : i * 192 + 192]
            rows = pl.ds(pl.multiple_of((2 * j + i) * ROWS, ROWS), ROWS)
            wide_q[rows, :LATENT] = dot(mine[:, :NOPE], w_key[2 * j + i]).astype(BF16)
            wide_q[rows, LATENT:] = jnp.concatenate([mine[:, NOPE:], one_hot], axis=1)
        return 0

    lax.fori_loop(0, HEADS // 2, absorb, 0)

    @pl.when(core == 0)
    def _():
        def mine(x_of, zh_of):
            return slab(x_of, zh_of, 0)

        def turned(k):
            return (x + k) % 4

        arrive(mine(x_down, zh))
        send(0, mine(x_down, zh), up, 0)
        send(0, mine(x_down, zh), outer)
        send(0, mine(x_down, zh), twin)
        arrive(mine(x_up, zh))
        send(0, mine(x_up, zh), down, 1)
        send(0, mine(x_up, zh), outer)
        send(0, mine(x_up, zh), twin)
        arrive(mine(x_far, zh), 0)
        arrive(mine(x_far, zh), 1)
        send(0, mine(x_far, zh), outer)
        send(0, mine(x_far, zh), twin)
        for k in (0, 3, 1, 2):
            arrive(mine(turned(k), zh_outer))
            send(0, mine(turned(k), zh_outer), inner)
            send(0, mine(turned(k), zh_outer), twin)
        for k in (zl, 3 - zl):
            arrive(mine(turned(k), zh_inner))
            send(0, mine(turned(k), zh_inner), outer)
            send(0, mine(turned(k), zh_inner), twin)
        for k in (1 - zl, 2 + zl):
            arrive(mine(turned(k), zh_inner))
            send(0, mine(turned(k), zh_inner), twin)
        for k in (1 - zl, 2 + zl):
            arrive(mine(turned(k), zh_far))
            send(0, mine(turned(k), zh_far), inner)
            send(0, mine(turned(k), zh_far), twin)
        for k in (zl, 3 - zl):
            arrive(mine(turned(k), zh_far))
            send(0, mine(turned(k), zh_far), twin)
        for x_of in range(4):
            for zh_of in range(4):
                arrive(slab(x_of, zh_of, 1))

    @pl.when(core == 1)
    def _():
        def mine(x_of, zh_of):
            return slab(x_of, zh_of, 1)

        arrive(mine(x, zh_outer))
        send(1, mine(x, zh_outer), inner)
        for device in (up, down, twin):
            send(1, mine(x, zh_outer), device)
        arrive(mine(x, zh_inner))
        send(1, mine(x, zh_inner), outer, zl)
        for device in (up, down, twin):
            send(1, mine(x, zh_inner), device)
        arrive(mine(x, zh_far), 1 - zl)
        send(1, mine(x, zh_far), inner, 1 - zl)
        arrive(mine(x, zh_far), zl)
        for device in (up, down, twin):
            send(1, mine(x, zh_far), device)
        for j, zh_of in enumerate((zh, zh_outer, zh_inner, zh_far)):
            arrive(mine(x_down, zh_of))
            if j < 2:
                send(1, mine(x_down, zh_of), up)
            send(1, mine(x_down, zh_of), twin)
            arrive(mine(x_up, zh_of))
            if j >= 2:
                send(1, mine(x_up, zh_of), down)
            send(1, mine(x_up, zh_of), twin)
        for zh_of in (zh, zh_outer, zh_inner, zh_far):
            arrive(mine(x_far, zh_of))
            send(1, mine(x_far, zh_of), twin)
        for x_of in range(4):
            for zh_of in range(4):
                arrive(slab(x_of, zh_of, 0))

    query_pos = my_slab * ROWS + row
    first_live = jnp.where(query_pos >= boundary, boundary, 0)

    def take(step, _):
        held = gathered[listed[step]]
        here = pl.ds(pl.multiple_of(step * ROWS, ROWS), ROWS)
        value[here, :] = held[:, :LATENT]
        key_t[:KEY, here] = held.T
        key_pos = (my_slab - step) * ROWS + column
        live = (key_pos >= first_live) & (key_pos <= query_pos)
        key_t[KEY:, here] = jnp.where(live, 0.0, NEGATIVE).astype(BF16)
        return 0

    lax.fori_loop(0, WINDOW, take, 0)
    loads[2].wait()

    scale = (NOPE + ROPE) ** -0.5 * LOG2E
    chunks = [pl.ds(i * CHUNK, CHUNK) for i in range(WINDOW * ROWS // CHUNK)]

    def score(q, chunk, slot, top):
        s = dot(q, key_t[:, chunk])
        scores[slot, :, chunk] = s
        for i in range(0, CHUNK, 128):
            part = s[:, i : i + 128]
            top = part if top is None else jnp.maximum(top, part)
        return top

    def q_rows(step):
        return wide_q[pl.ds(pl.multiple_of(step * PAIR, PAIR), PAIR), :]

    def attend(step, slot, ahead):
        top = jnp.max(tops[slot], axis=1, keepdims=True) * scale
        context, total, next_top = jnp.zeros((PAIR, LATENT), F32), jnp.zeros((PAIR, 128), F32), None
        for chunk in chunks:
            if ahead:
                next_top = score(q_rows(step + 1), chunk, 1 - slot, next_top)
            weights = jnp.exp2(scores[slot, :, chunk] * scale - top)
            for i in range(0, CHUNK, 128):
                total = total + weights[:, i : i + 128]
            context = context + dot(weights.astype(BF16), value[chunk, :])
        if ahead:
            tops[1 - slot] = next_top
        context = (context / jnp.sum(total, axis=1, keepdims=True)).astype(BF16)
        for i in range(2):
            h = 2 * step + i
            attended[:, pl.ds(pl.multiple_of(h * VHEAD, VHEAD), VHEAD)] = dot(
                context[i * ROWS : (i + 1) * ROWS], w_value[h]
            ).astype(BF16)
        for i in range(7):
            deliver(step, i).start()

    def columns_of(who, step):
        return pl.ds(pl.multiple_of(who * (HEADS * VHEAD) + step * PAIR, PAIR), PAIR)

    def deliver(step, i):
        mate = mates[i][1]
        return pltpu.make_async_remote_copy(
            src_ref=attended.at[pl.ds(pl.multiple_of(mate * 16, 16), 16), columns_of(0, step)],
            dst_ref=out.at[:, columns_of(head, step)],
            send_sem=out_send.at[step, i], recv_sem=out_recv.at[step, i],
            device_id=mates[i], device_id_type=MESH,
        )

    top = None
    for chunk in chunks:
        top = score(q_rows(0), chunk, 0, top)
    tops[0] = top

    def two_steps(i, _):
        attend(2 * i, 0, True)
        attend(2 * i + 1, 1, True)
        return 0

    lax.fori_loop(0, STEPS // 2 - 1, two_steps, 0)
    attend(STEPS - 2, 0, True)
    attend(STEPS - 1, 1, False)

    out[:, pl.ds(pl.multiple_of(head * (HEADS * VHEAD), 128), HEADS * VHEAD)] = attended[
        pl.ds(pl.multiple_of(head * 16, 16), 16), :
    ]

    for which in range(2):

        @pl.when(core == which)
        def _(which=which):
            for number, half in enumerate(sent[which]):
                transfer(seq, twin, number, None if half is None else 0).wait_send()

    def finish(step, _):
        for i in range(7):
            deliver(step, i).wait_send()
            sender = (head + 7 - i) % 8
            pltpu.make_async_remote_copy(
                src_ref=attended.at[pl.ds(0, 16), columns_of(0, step)],
                dst_ref=out.at[:, columns_of(sender, step)],
                send_sem=out_send.at[step, i], recv_sem=out_recv.at[step, i],
                device_id=mates[i], device_id_type=MESH,
            ).wait_recv()
        return 0

    lax.fori_loop(0, STEPS, finish, 0)


def shards(queries, latent_keys, w_key_up, w_value_up, slab_order, segment_ids):
    keys = WINDOW * ROWS
    return pl.pallas_call(
        kernel,
        out_shape=jax.ShapeDtypeStruct((16, 8 * HEADS * VHEAD), BF16),
        in_specs=[
            pl.BlockSpec(memory_space=pltpu.SMEM),
            pl.BlockSpec(memory_space=pltpu.SMEM),
            pl.BlockSpec(memory_space=pltpu.VMEM),
            pl.BlockSpec(memory_space=pl.ANY),
            pl.BlockSpec(memory_space=pl.ANY),
            pl.BlockSpec(memory_space=pl.ANY),
        ],
        out_specs=pl.BlockSpec(memory_space=pltpu.VMEM),
        scratch_shapes=[
            pltpu.VMEM((SLABS, ROWS, KEY), BF16),
            pltpu.VMEM((HEADS * ROWS, WIDE), BF16),
            pltpu.VMEM((WIDE, keys), BF16),
            pltpu.VMEM((keys, LATENT), BF16),
            pltpu.VMEM((2, PAIR, keys), F32),
            pltpu.VMEM((2, PAIR, 128), F32),
            pltpu.VMEM((ROWS, HEADS * VHEAD), BF16),
            pltpu.VMEM((ROWS, HEADS * (NOPE + ROPE)), BF16),
            pltpu.VMEM((HEADS, NOPE, LATENT), BF16),
            pltpu.VMEM((HEADS, LATENT, VHEAD), BF16),
            pltpu.SMEM((WINDOW,), jnp.int32),
            pltpu.SemaphoreType.DMA((3,)),
            pltpu.SemaphoreType.DMA((32,)),
            pltpu.SemaphoreType.DMA((SLABS,)),
            pltpu.SemaphoreType.DMA((2,)),
            pltpu.SemaphoreType.DMA((STEPS, 7)),
            pltpu.SemaphoreType.DMA((STEPS, 7)),
        ],
        compiler_params=pltpu.CompilerParams(
            collective_id=0, has_side_effects=True, vmem_limit_bytes=56 * 2**20
        ),
        cost_estimate=pl.CostEstimate(
            flops=16 * 10**9, bytes_accessed=6 * 2**20, transcendentals=6 * 10**6
        ),
    )(slab_order, segment_ids, latent_keys, queries, w_key_up, w_value_up)


def solution(mesh):
    in_specs = (
        P("seq", "head"),
        P("seq", None),
        P("head", None, None),
        P("head", None, None),
        P(),
        P(),
    )
    out_specs = P(("seq", "head"), None)
    return jax.shard_map(shards, mesh=mesh, in_specs=in_specs, out_specs=out_specs, check_vma=False)
```

time: 247 us -> 75.1 us (0.30)
  the two profiles are of different devices: /device:TPU:195 before, /device:TPU:1 now
where the time goes in v1:
time: 75.1 us; the launch traced here: 74.9 us
  Pallas kernels  71.4 us (95%)
  local copies, waits for them, and re-layouts  3.58 us (5%)
    pallas_call x1, Pallas kernels, shards(): pl.pallas_call(kernel, out_shape=jax.ShapeDtypeStruct((16, 8 * HEADS * VH...  71.4 us
    unnamed x2, local copies, waits for them, and re-layouts  3.58 us

profile of v1, /device:TPU:1, one launch (start us, length us, event | category | flops | bytes accessed | tf_op | source)
XLA Modules:
  0.0 74.9 jit_solution(15752014337507294400)
XLA Ops:
  0.0 1.7 %copy.7.latent = bf16[128,576]{1,0:T(8,128)(2,1)} copy(bf16[128,576]{0,1:T(8,128)(2,1)} %param.7) | data formatting | bytes 294912 | tf_op args[1]
  1.7 71.4 %shard_map.64 = bf16[16,16384]{1,0:T(8,128)(2,1)} custom-call(s32[32]{0:T(128)} %order.1, s32[4096]{0:T(1024)} %segment.1, bf16[128,576]{1,0:T(8,128)(2,1)} %copy.7.latent, bf16[128,3072]{1,0:T(8,128)(2,1)} %queries_hbm.1, bf16[16,128,512]{2,1,0:T(8,128)(2,1)} %w_key_hbm.1, bf16[16,512,128]{2,1,0:T(8,128)(2,1)} %w_value_hbm.1), custom_call_target="tpu_custom_call" | custom-call | flops 16000000000 | bytes 6291456 | tf_op jit(solution)/shard_map/pallas_call | solution.py:319
  73.1 1.9 %copy.9 = bf16[16,16384]{1,0:T(8,128)(2,1)} copy(bf16[16,16384]{1,0:T(8,128)(2,1)} %shard_map.64) | data formatting | bytes 1048576

commit v2 on v1

v2 whole, which is shorter than its diff:
```python
import functools

import jax
import jax.numpy as jnp
from jax import lax
from jax.experimental import pallas as pl
from jax.experimental.pallas import tpu as pltpu
from jax.sharding import PartitionSpec as P

MESH = pl.DeviceIdType.MESH
BF16 = jnp.bfloat16
F32 = jnp.float32

HEADS = 16
ROWS = 128
NOPE, ROPE, LATENT, VHEAD = 128, 64, 512, 128
KEY = LATENT + ROPE
HALF = KEY // 2
WIDE = KEY + ROWS
SLABS = 32
BAND = 8
PAIR = 2 * ROWS
STEPS = HEADS // 2
CHUNK = 256
NEGATIVE = -1.0e30
LOG2E = 1.4426950408889634


def dot(a, b):
    return jnp.dot(a, b, preferred_element_type=F32)


def kernel(
    order, segment, latent, queries_hbm, w_key_hbm, w_value_hbm, out,
    own_band, outer_band, inner_band, far_band, wide_q, value, scores, tops, best, total, context,
    attended, queries, w_key, w_value, load_sem, send_sem, recv_sem, out_send, out_recv,
):
    seq, head = lax.axis_index("seq"), lax.axis_index("head")
    core, zh, x = seq % 2, (seq // 2) % 4, seq // 8
    y, zl = head % 4, head // 4

    def slab(x_of, zh_of, core_of):
        return (x_of * 4 + zh_of) * 2 + core_of

    x_up, x_down, x_far = (x + 1) % 4, (x + 3) % 4, (x + 2) % 4
    zh_outer = (zh + 3 + 2 * zl) % 4
    zh_inner = (zh + 5 - 2 * zl) % 4
    zh_far = (zh + 2) % 4
    up = (slab(x_up, zh, core), head)
    down = (slab(x_down, zh, core), head)
    outer = (slab(x, zh_outer, core), (1 - zl) * 4 + y)
    inner = (seq, (1 - zl) * 4 + y)
    twin = (slab(x, zh, 1 - core), head)
    y_up = (seq, zl * 4 + (y + 1) % 4)
    y_down = (seq, zl * 4 + (y + 3) % 4)
    mates = [(seq, (head + 1 + i) % 8) for i in range(7)]

    loads = [
        pltpu.make_async_copy(queries_hbm, queries, load_sem.at[0]),
        pltpu.make_async_copy(w_key_hbm, w_key, load_sem.at[1]),
        pltpu.make_async_copy(w_value_hbm, w_value, load_sem.at[2]),
    ]
    for load in loads:
        load.start()
    bands = (own_band, outer_band, inner_band, far_band)
    own_band[x * 2 + core, :KEY] = latent[...]

    barrier = pltpu.get_barrier_semaphore()
    greeted = [up, down, outer, twin] + mates
    for device in greeted:
        pl.semaphore_signal(barrier, inc=1, device_id=device, device_id_type=MESH)
    pl.semaphore_wait(barrier, len(greeted))

    def transfer(band, landing, k, half, device, sent, core_of):
        place = ((x + k) % 4) * 2 + core_of
        span = pl.ds(pl.multiple_of(half * HALF, 16), HALF)
        return pltpu.make_async_remote_copy(
            src_ref=bands[band].at[place, span], dst_ref=bands[landing].at[place, span],
            send_sem=send_sem.at[sent], recv_sem=recv_sem.at[landing, place, half],
            device_id=device, device_id_type=MESH,
        )

    sent = []

    def send(band, landing, k, half, *devices):
        for device in devices:
            transfer(band, landing, k, half, device, len(sent), core).start()
            sent.append(device)

    def arrive(band, k, half, core_of=core):
        transfer(band, band, k, half, twin, 0, core_of).wait_recv()

    kept, other = y % 2, 1 - y % 2
    for half in range(2):
        send(0, 0, 0, half, up, down)
    send(0, 1, 0, kept, outer)
    for half in range(2):
        send(0, 0, 0, half, twin)

    def search(_, span):
        low, high = span
        middle = (low + high) // 2
        first = segment[middle] == 0
        return jnp.where(first, middle + 1, low), jnp.where(first, high, middle)

    boundary, _ = lax.fori_loop(0, 12, search, (0, SLABS * ROWS - 1))
    my_slab = order[seq]

    loads[0].wait()
    loads[1].wait()
    row = lax.broadcasted_iota(jnp.int32, (ROWS, ROWS), 0)
    column = lax.broadcasted_iota(jnp.int32, (ROWS, ROWS), 1)
    one_hot = (row == column).astype(BF16)

    def absorb(j, _):
        two = queries[:, pl.ds(pl.multiple_of(j * 384, 384), 384)]
        for i in range(2):
            mine = two[:, i * 192 : i * 192 + 192]
            rows = pl.ds(pl.multiple_of((2 * j + i) * ROWS, ROWS), ROWS)
            wide_q[rows, :LATENT] = dot(mine[:, :NOPE], w_key[2 * j + i]).astype(BF16)
            wide_q[rows, LATENT:] = jnp.concatenate([mine[:, NOPE:], one_hot], axis=1)
        return 0

    lax.fori_loop(0, HEADS // 2, absorb, 0)

    query_pos = my_slab * ROWS + row
    first_live = jnp.where(query_pos >= boundary, boundary, 0)

    def cover(place, _):
        for band, zh_of in enumerate((zh, zh_outer, zh_inner, zh_far)):
            key_pos = order[slab(place // 2, zh_of, place % 2)] * ROWS + column
            live = (key_pos >= first_live) & (key_pos <= query_pos)
            bands[band][place, KEY:] = jnp.where(live, 0.0, NEGATIVE).astype(BF16)
        return 0

    lax.fori_loop(0, BAND, cover, 0)

    sideways = {0: y_up, 3: y_up, 1: y_down, 2: y_down}

    def along_x(k, onward, passed):
        arrive(0, k, 0)
        arrive(0, k, 1)
        if onward is not None:
            send(0, 0, k, passed, onward)
        send(0, 1, k, kept, outer)
        for half in range(2):
            send(0, 0, k, half, twin)

    def from_outer(k):
        arrive(1, k, kept)
        send(1, 2, k, kept, inner)
        send(1, 1, k, kept, sideways[k], twin)

    def from_inner(k):
        arrive(2, k, kept)
        send(2, 2, k, kept, sideways[k], twin)

    def far_outer(k, side):
        arrive(3, k, kept)
        send(3, 3, k, kept, inner, side, twin)

    def far_inner(k, side):
        arrive(3, k, kept)
        send(3, 3, k, kept, side, twin)

    def from_side(band, k):
        arrive(band, k, other)
        send(band, band, k, other, twin)

    def complete(band):
        for k in range(4):
            for half in range(2):
                arrive(band, k, half, 1 - core)

    along_x(3, up, 0)
    along_x(1, down, 1)
    from_outer(0)
    along_x(2, None, None)
    from_inner(0)
    complete(0)

    def during_own(step):
        if step == 0:
            from_outer(3)
        elif step == 1:
            from_outer(1)
            from_outer(2)
        elif step == 2:
            from_inner(3)
            send(2, 3, 3 * zl, kept, outer)
        elif step == 3:
            from_inner(1)
            from_inner(2)
            send(2, 3, 1 + zl, kept, outer)
            from_side(1, 0)
        elif step == 4:
            from_side(1, 3)
            from_side(1, 1)
            from_side(1, 2)
        elif step == 5:
            from_side(2, 0)
        elif step == 6:
            far_outer(3 - 3 * zl, y_up)

    def during_outer(step):
        if step == 0:
            far_outer(2 - zl, y_down)
            from_side(2, 3)
        elif step == 1:
            from_side(2, 1)
            from_side(2, 2)
        elif step == 2:
            far_inner(3 * zl, y_up)
        elif step == 3:
            far_inner(1 + zl, y_down)
        elif step == 4:
            from_side(3, 3 - 3 * zl)
        elif step == 5:
            from_side(3, 2 - zl)
        elif step == 6:
            from_side(3, 3 * zl)

    def during_inner(step):
        if step == 0:
            from_side(3, 1 + zl)

    scale = (NOPE + ROPE) ** -0.5 * LOG2E
    parts = range(0, BAND * ROWS, CHUNK)

    def rows_of(step):
        return pl.ds(pl.multiple_of(step * PAIR, PAIR), PAIR)

    def score(band, q, first, slot, top):
        keys = jnp.concatenate(
            [bands[band][(first + i) // ROWS] for i in range(0, CHUNK, ROWS)], axis=1
        )
        s = dot(q, keys)
        scores[slot, :, pl.ds(first, CHUNK)] = s
        for i in range(0, CHUNK, 128):
            part = s[:, i : i + 128]
            top = part if top is None else jnp.maximum(top, part)
        return top

    def attend(band, step, ahead):
        slot = step % 2
        here = rows_of(step)
        top = jnp.broadcast_to(jnp.max(tops[slot], axis=1, keepdims=True), (PAIR, 128)) * scale
        if band == 0:
            so_far, sums = jnp.zeros((PAIR, LATENT), F32), jnp.zeros((PAIR, 128), F32)
        else:
            before = best[here, :]
            top = jnp.maximum(top, before)
            fade = jnp.exp2(before - top)
            sums = total[here, :] * fade
            so_far = None
        gained, next_top = None, None
        for first in parts:
            if ahead:
                next_top = score(band, wide_q[rows_of(step + 1), :], first, 1 - slot, next_top)
            weights = []
            for i in range(0, CHUNK, 128):
                w = jnp.exp2(scores[slot, :, pl.ds(first + i, 128)] * scale - top)
                sums = sums + w
                weights.append(w.astype(BF16))
            more = dot(jnp.concatenate(weights, axis=1), value[pl.ds(first, CHUNK), :])
            gained = more if gained is None else gained + more
        if ahead:
            tops[1 - slot] = next_top
        if band > 0:
            gained = gained + context[here, :] * jnp.concatenate([fade] * 4, axis=1)
        if band < 3:
            best[here, :] = top
            total[here, :] = sums
            context[here, :] = gained
            return
        finished = (gained / jnp.sum(sums, axis=1, keepdims=True)).astype(BF16)
        for i in range(2):
            h = 2 * step + i
            attended[:, pl.ds(pl.multiple_of(h * VHEAD, VHEAD), VHEAD)] = dot(
                finished[i * ROWS : (i + 1) * ROWS], w_value[h]
            ).astype(BF16)
        for i in range(7):
            deliver(step, i).start()

    def columns_of(who, step):
        return pl.ds(pl.multiple_of(who * (HEADS * VHEAD) + step * PAIR, PAIR), PAIR)

    def deliver(step, i):
        mate = mates[i][1]
        return pltpu.make_async_remote_copy(
            src_ref=attended.at[pl.ds(pl.multiple_of(mate * 16, 16), 16), columns_of(0, step)],
            dst_ref=out.at[:, columns_of(head, step)],
            send_sem=out_send.at[step, i], recv_sem=out_recv.at[step, i],
            device_id=mates[i], device_id_type=MESH,
        )

    for band, between in enumerate((during_own, during_outer, during_inner, None)):
        if band > 0:
            complete(band)
        if band == 3:
            loads[2].wait()

        def turn(place, _, band=band):
            value[pl.ds(pl.multiple_of(place * ROWS, ROWS), ROWS), :] = bands[band][place, :LATENT].T
            return 0

        lax.fori_loop(0, BAND, turn, 0)
        top = None
        for first in parts:
            top = score(band, wide_q[rows_of(0), :], first, 0, top)
        tops[0] = top

        def go(step, _, band=band, between=between):
            attend(band, step, True)
            if between is not None:
                for n in range(STEPS - 1):

                    @pl.when(step == n)
                    def _(n=n):
                        between(n)

            return 0

        lax.fori_loop(0, STEPS - 1, go, 0)
        attend(band, STEPS - 1, False)

    out[:, pl.ds(pl.multiple_of(head * (HEADS * VHEAD), 128), HEADS * VHEAD)] = attended[
        pl.ds(pl.multiple_of(head * 16, 16), 16), :
    ]
    for number in range(len(sent)):
        transfer(0, 0, 0, 0, twin, number, core).wait_send()

    def finish(step, _):
        for i in range(7):
            deliver(step, i).wait_send()
            sender = (head + 7 - i) % 8
            pltpu.make_async_remote_copy(
                src_ref=attended.at[pl.ds(0, 16), columns_of(0, step)],
                dst_ref=out.at[:, columns_of(sender, step)],
                send_sem=out_send.at[step, i], recv_sem=out_recv.at[step, i],
                device_id=mates[i], device_id_type=MESH,
            ).wait_recv()
        return 0

    lax.fori_loop(0, STEPS, finish, 0)


def shards(queries, latent_keys, w_key_up, w_value_up, slab_order, segment_ids):
    rows = HEADS * ROWS
    return pl.pallas_call(
        kernel,
        out_shape=jax.ShapeDtypeStruct((16, 8 * HEADS * VHEAD), BF16),
        in_specs=[
            pl.BlockSpec(memory_space=pltpu.SMEM),
            pl.BlockSpec(memory_space=pltpu.SMEM),
            pl.BlockSpec(memory_space=pltpu.VMEM),
            pl.BlockSpec(memory_space=pl.ANY),
            pl.BlockSpec(memory_space=pl.ANY),
            pl.BlockSpec(memory_space=pl.ANY),
        ],
        out_specs=pl.BlockSpec(memory_space=pltpu.VMEM),
        scratch_shapes=[
            pltpu.VMEM((BAND, WIDE, ROWS), BF16),
            pltpu.VMEM((BAND, WIDE, ROWS), BF16),
            pltpu.VMEM((BAND, WIDE, ROWS), BF16),
            pltpu.VMEM((BAND, WIDE, ROWS), BF16),
            pltpu.VMEM((rows, WIDE), BF16),
            pltpu.VMEM((BAND * ROWS, LATENT), BF16),
            pltpu.VMEM((2, PAIR, BAND * ROWS), F32),
            pltpu.VMEM((2, PAIR, 128), F32),
            pltpu.VMEM((rows, 128), F32),
            pltpu.VMEM((rows, 128), F32),
            pltpu.VMEM((rows, LATENT), F32),
            pltpu.VMEM((ROWS, HEADS * VHEAD), BF16),
            pltpu.VMEM((ROWS, HEADS * (NOPE + ROPE)), BF16),
            pltpu.VMEM((HEADS, NOPE, LATENT), BF16),
            pltpu.VMEM((HEADS, LATENT, VHEAD), BF16),
            pltpu.SemaphoreType.DMA((3,)),
            pltpu.SemaphoreType.DMA((64,)),
            pltpu.SemaphoreType.DMA((4, BAND, 2)),
            pltpu.SemaphoreType.DMA((STEPS, 7)),
            pltpu.SemaphoreType.DMA((STEPS, 7)),
        ],
        compiler_params=pltpu.CompilerParams(
            collective_id=0, has_side_effects=True, vmem_limit_bytes=56 * 2**20
        ),
        cost_estimate=pl.CostEstimate(
            flops=20 * 10**9, bytes_accessed=6 * 2**20, transcendentals=8 * 10**6
        ),
    )(slab_order, segment_ids, latent_keys.T, queries, w_key_up, w_value_up)


def solution(mesh):
    in_specs = (
        P("seq", "head"),
        P("seq", None),
        P("head", None, None),
        P("head", None, None),
        P(),
        P(),
    )
    out_specs = P(("seq", "head"), None)
    return jax.shard_map(shards, mesh=mesh, in_specs=in_specs, out_specs=out_specs, check_vma=False)
```

time: 75.1 us -> 88.9 us (1.18)
  Pallas kernels: 71.4 us -> 86.9 us
  local copies, waits for them, and re-layouts: 3.58 us -> 1.87 us
    pallas_call x1, Pallas kernels: 71.4 us -> 86.9 us  [shards(): pl.pallas_call(kernel, out_shape=jax.ShapeDtypeStruct((16, 8 * HEADS * VH...]
    unnamed x2 -> x1, local copies, waits for them, and re-layouts: 3.58 us -> 1.87 us
where the time goes in v2:
time: 88.9 us; the launch traced here: 88.8 us
  Pallas kernels  86.9 us (98%)
  local copies, waits for them, and re-layouts  1.87 us (2%)
    pallas_call x1, Pallas kernels, shards(): pl.pallas_call(kernel, out_shape=jax.ShapeDtypeStruct((16, 8 * HEADS * VH...  86.9 us
    unnamed x1, local copies, waits for them, and re-layouts  1.87 us

profile of v2, /device:TPU:1, one launch (start us, length us, event | category | flops | bytes accessed | tf_op | source)
XLA Modules:
  0.0 88.8 jit_solution(8182025118197349654)
XLA Ops:
  0.0 86.9 %shard_map.64 = bf16[16,16384]{1,0:T(8,128)(2,1)} custom-call(s32[32]{0:T(128)} %order.1, s32[4096]{0:T(1024)} %segment.1, bf16[576,128]{1,0:T(8,128)(2,1)} %bitcast.1, bf16[128,3072]{1,0:T(8,128)(2,1)} %queries_hbm.1, bf16[16,128,512]{2,1,0:T(8,128)(2,1)} %w_key_hbm.1, bf16[16,512,128]{2,1,0:T(8,128)(2,1)} %w_value_hbm.1), custom_call_target="tpu_custom_call" | custom-call | flops 20000000000 | bytes 6291456 | tf_op jit(solution)/shard_map/pallas_call | solution.py:350
  86.9 1.9 %copy.8 = bf16[16,16384]{1,0:T(8,128)(2,1)} copy(bf16[16,16384]{1,0:T(8,128)(2,1)} %shard_map.64) | data formatting | bytes 1048576

commit v3 on v2

--- a/solution.py
+++ b/solution.py
@@ -32,7 +32,7 @@
 
 def kernel(
     order, segment, latent, queries_hbm, w_key_hbm, w_value_hbm, out,
-    own_band, outer_band, inner_band, far_band, wide_q, value, scores, tops, best, total, context,
+    own_band, outer_band, inner_band, far_band, wide_q, value, scores_0, scores_1, tops_0, tops_1, best, total, context,
     attended, queries, w_key, w_value, load_sem, send_sem, recv_sem, out_send, out_recv,
 ):
     seq, head = lax.axis_index("seq"), lax.axis_index("head")
@@ -225,6 +225,7 @@
             from_side(3, 1 + zl)
 
     scale = (NOPE + ROPE) ** -0.5 * LOG2E
+    scores, tops = (scores_0, scores_1), (tops_0, tops_1)
     parts = range(0, BAND * ROWS, CHUNK)
 
     def rows_of(step):
@@ -235,16 +236,15 @@
             [bands[band][(first + i) // ROWS] for i in range(0, CHUNK, ROWS)], axis=1
         )
         s = dot(q, keys)
-        scores[slot, :, pl.ds(first, CHUNK)] = s
+        scores[slot][:, pl.ds(first, CHUNK)] = s
         for i in range(0, CHUNK, 128):
             part = s[:, i : i + 128]
             top = part if top is None else jnp.maximum(top, part)
         return top
 
-    def attend(band, step, ahead):
-        slot = step % 2
+    def attend(band, step, slot, ahead):
         here = rows_of(step)
-        top = jnp.broadcast_to(jnp.max(tops[slot], axis=1, keepdims=True), (PAIR, 128)) * scale
+        top = jnp.broadcast_to(jnp.max(tops[slot][...], axis=1, keepdims=True), (PAIR, 128)) * scale
         if band == 0:
             so_far, sums = jnp.zeros((PAIR, LATENT), F32), jnp.zeros((PAIR, 128), F32)
         else:
@@ -259,13 +259,13 @@
                 next_top = score(band, wide_q[rows_of(step + 1), :], first, 1 - slot, next_top)
             weights = []
             for i in range(0, CHUNK, 128):
-                w = jnp.exp2(scores[slot, :, pl.ds(first + i, 128)] * scale - top)
+                w = jnp.exp2(scores[slot][:, pl.ds(first + i, 128)] * scale - top)
                 sums = sums + w
                 weights.append(w.astype(BF16))
             more = dot(jnp.concatenate(weights, axis=1), value[pl.ds(first, CHUNK), :])
             gained = more if gained is None else gained + more
         if ahead:
-            tops[1 - slot] = next_top
+            tops[1 - slot][...] = next_top
         if band > 0:
             gained = gained + context[here, :] * jnp.concatenate([fade] * 4, axis=1)
         if band < 3:
@@ -308,21 +308,25 @@
         top = None
         for first in parts:
             top = score(band, wide_q[rows_of(0), :], first, 0, top)
-        tops[0] = top
-
-        def go(step, _, band=band, between=between):
-            attend(band, step, True)
-            if between is not None:
-                for n in range(STEPS - 1):
-
-                    @pl.when(step == n)
-                    def _(n=n):
-                        between(n)
+        tops[0][...] = top
+
+        def go(i, _, band=band, between=between):
+            for slot in range(2):
+                attend(band, 2 * i + slot, slot, True)
+                for n in range(slot, STEPS - 2, 2):
+                    if between is not None:
+
+                        @pl.when(i == n // 2)
+                        def _(n=n):
+                            between(n)
 
             return 0
 
-        lax.fori_loop(0, STEPS - 1, go, 0)
-        attend(band, STEPS - 1, False)
+        lax.fori_loop(0, STEPS // 2 - 1, go, 0)
+        attend(band, STEPS - 2, 0, True)
+        if between is not None:
+            between(STEPS - 2)
+        attend(band, STEPS - 1, 1, False)
 
     out[:, pl.ds(pl.multiple_of(head * (HEADS * VHEAD), 128), HEADS * VHEAD)] = attended[
         pl.ds(pl.multiple_of(head * 16, 16), 16), :
@@ -366,8 +370,10 @@
             pltpu.VMEM((BAND, WIDE, ROWS), BF16),
             pltpu.VMEM((rows, WIDE), BF16),
             pltpu.VMEM((BAND * ROWS, LATENT), BF16),
-            pltpu.VMEM((2, PAIR, BAND * ROWS), F32),
-            pltpu.VMEM((2, PAIR, 128), F32),
+            pltpu.VMEM((PAIR, BAND * ROWS), F32),
+            pltpu.VMEM((PAIR, BAND * ROWS), F32),
+            pltpu.VMEM((PAIR, 128), F32),
+            pltpu.VMEM((PAIR, 128), F32),
             pltpu.VMEM((rows, 128), F32),
             pltpu.VMEM((rows, 128), F32),
             pltpu.VMEM((rows, LATENT), F32),

time: 88.9 us -> 65.7 us (0.74)
  Pallas kernels: 86.9 us -> 63.7 us
    pallas_call x1, Pallas kernels: 86.9 us -> 63.7 us  [shards(): pl.pallas_call(kernel, out_shape=jax.ShapeDtypeStruct((16, 8 * HEADS * VH...]
where the time goes in v3:
time: 65.7 us; the launch traced here: 65.6 us
  Pallas kernels  63.7 us (97%)
  local copies, waits for them, and re-layouts  1.87 us (3%)
    pallas_call x1, Pallas kernels, shards(): pl.pallas_call(kernel, out_shape=jax.ShapeDtypeStruct((16, 8 * HEADS * VH...  63.7 us
    unnamed x1, local copies, waits for them, and re-layouts  1.87 us

profile of v3, /device:TPU:1, one launch (start us, length us, event | category | flops | bytes accessed | tf_op | source)
XLA Modules:
  0.0 65.6 jit_solution(7243558940343377396)
XLA Ops:
  0.0 63.7 %shard_map.64 = bf16[16,16384]{1,0:T(8,128)(2,1)} custom-call(s32[32]{0:T(128)} %order.1, s32[4096]{0:T(1024)} %segment.1, bf16[576,128]{1,0:T(8,128)(2,1)} %bitcast.1, bf16[128,3072]{1,0:T(8,128)(2,1)} %queries_hbm.1, bf16[16,128,512]{2,1,0:T(8,128)(2,1)} %w_key_hbm.1, bf16[16,512,128]{2,1,0:T(8,128)(2,1)} %w_value_hbm.1), custom_call_target="tpu_custom_call" | custom-call | flops 20000000000 | bytes 6291456 | tf_op jit(solution)/shard_map/pallas_call | solution.py:354
  63.7 1.9 %copy.8 = bf16[16,16384]{1,0:T(8,128)(2,1)} copy(bf16[16,16384]{1,0:T(8,128)(2,1)} %shard_map.64) | data formatting | bytes 1048576

commit v4 on v3

--- a/solution.py
+++ b/solution.py
@@ -15,7 +15,7 @@
 ROWS = 128
 NOPE, ROPE, LATENT, VHEAD = 128, 64, 512, 128
 KEY = LATENT + ROPE
-HALF = KEY // 2
+QUARTER = KEY // 4
 WIDE = KEY + ROWS
 SLABS = 32
 BAND = 8
@@ -50,6 +50,7 @@
     down = (slab(x_down, zh, core), head)
     outer = (slab(x, zh_outer, core), (1 - zl) * 4 + y)
     inner = (seq, (1 - zl) * 4 + y)
+    beyond = (slab(x, zh_far, core), (1 - zl) * 4 + y)
     twin = (slab(x, zh, 1 - core), head)
     y_up = (seq, zl * 4 + (y + 1) % 4)
     y_down = (seq, zl * 4 + (y + 3) % 4)
@@ -63,39 +64,40 @@
     for load in loads:
         load.start()
     bands = (own_band, outer_band, inner_band, far_band)
-    own_band[x * 2 + core, :KEY] = latent[...]
+    own_band[core, :KEY] = latent[...]
 
     barrier = pltpu.get_barrier_semaphore()
-    greeted = [up, down, outer, twin] + mates
+    greeted = [up, down, outer, beyond, twin] + mates
     for device in greeted:
         pl.semaphore_signal(barrier, inc=1, device_id=device, device_id_type=MESH)
     pl.semaphore_wait(barrier, len(greeted))
 
-    def transfer(band, landing, k, half, device, sent, core_of):
-        place = ((x + k) % 4) * 2 + core_of
-        span = pl.ds(pl.multiple_of(half * HALF, 16), HALF)
+    def transfer(band, landing, k, first, length, device, sent, core_of):
+        there = (k + (3 if device is up else 1 if device is down else 0)) % 4
+        span = pl.ds(pl.multiple_of(first * QUARTER, 16), length * QUARTER)
         return pltpu.make_async_remote_copy(
-            src_ref=bands[band].at[place, span], dst_ref=bands[landing].at[place, span],
-            send_sem=send_sem.at[sent], recv_sem=recv_sem.at[landing, place, half],
+            src_ref=bands[band].at[2 * k + core_of, span],
+            dst_ref=bands[landing].at[2 * there + core_of, span],
+            send_sem=send_sem.at[sent], recv_sem=recv_sem.at[landing, 2 * there + core_of, first],
             device_id=device, device_id_type=MESH,
         )
 
     sent = []
 
-    def send(band, landing, k, half, *devices):
+    def send(band, landing, k, first, length, *devices):
         for device in devices:
-            transfer(band, landing, k, half, device, len(sent), core).start()
-            sent.append(device)
-
-    def arrive(band, k, half, core_of=core):
-        transfer(band, band, k, half, twin, 0, core_of).wait_recv()
-
-    kept, other = y % 2, 1 - y % 2
-    for half in range(2):
-        send(0, 0, 0, half, up, down)
-    send(0, 1, 0, kept, outer)
-    for half in range(2):
-        send(0, 0, 0, half, twin)
+            transfer(band, landing, k, first, length, device, len(sent), core).start()
+            sent.append(length)
+
+    def arrive(band, k, first, length, core_of=core):
+        transfer(band, band, k, first, length, twin, 0, core_of).wait_recv()
+
+    kept, other = 2 * (y % 2), 2 - 2 * (y % 2)
+    for half in (0, 2):
+        send(0, 0, 0, half, 2, up, down)
+        send(0, 1, 0, half, 2, outer)
+    send(0, 3, 0, 2 * zl, 2, beyond)
+    send(0, 0, 0, 0, 4, twin)
 
     def search(_, span):
         low, high = span
@@ -128,101 +130,99 @@
 
     def cover(place, _):
         for band, zh_of in enumerate((zh, zh_outer, zh_inner, zh_far)):
-            key_pos = order[slab(place // 2, zh_of, place % 2)] * ROWS + column
+            key_pos = order[slab((x + place // 2) % 4, zh_of, place % 2)] * ROWS + column
             live = (key_pos >= first_live) & (key_pos <= query_pos)
             bands[band][place, KEY:] = jnp.where(live, 0.0, NEGATIVE).astype(BF16)
         return 0
 
     lax.fori_loop(0, BAND, cover, 0)
 
-    sideways = {0: y_up, 3: y_up, 1: y_down, 2: y_down}
-
-    def along_x(k, onward, passed):
-        arrive(0, k, 0)
-        arrive(0, k, 1)
-        if onward is not None:
-            send(0, 0, k, passed, onward)
-        send(0, 1, k, kept, outer)
-        for half in range(2):
-            send(0, 0, k, half, twin)
-
-    def from_outer(k):
-        arrive(1, k, kept)
-        send(1, 2, k, kept, inner)
-        send(1, 1, k, kept, sideways[k], twin)
-
-    def from_inner(k):
-        arrive(2, k, kept)
-        send(2, 2, k, kept, sideways[k], twin)
-
-    def far_outer(k, side):
-        arrive(3, k, kept)
-        send(3, 3, k, kept, inner, side, twin)
-
-    def far_inner(k, side):
-        arrive(3, k, kept)
-        send(3, 3, k, kept, side, twin)
-
-    def from_side(band, k):
-        arrive(band, k, other)
-        send(band, band, k, other, twin)
-
-    def complete(band):
-        for k in range(4):
-            for half in range(2):
-                arrive(band, k, half, 1 - core)
-
-    along_x(3, up, 0)
-    along_x(1, down, 1)
-    from_outer(0)
-    along_x(2, None, None)
-    from_inner(0)
-    complete(0)
-
-    def during_own(step):
-        if step == 0:
-            from_outer(3)
-        elif step == 1:
-            from_outer(1)
-            from_outer(2)
-        elif step == 2:
-            from_inner(3)
-            send(2, 3, 3 * zl, kept, outer)
-        elif step == 3:
-            from_inner(1)
-            from_inner(2)
-            send(2, 3, 1 + zl, kept, outer)
-            from_side(1, 0)
-        elif step == 4:
-            from_side(1, 3)
-            from_side(1, 1)
-            from_side(1, 2)
-        elif step == 5:
-            from_side(2, 0)
-        elif step == 6:
-            far_outer(3 - 3 * zl, y_up)
-
-    def during_outer(step):
-        if step == 0:
-            far_outer(2 - zl, y_down)
-            from_side(2, 3)
-        elif step == 1:
-            from_side(2, 1)
-            from_side(2, 2)
-        elif step == 2:
-            far_inner(3 * zl, y_up)
-        elif step == 3:
-            far_inner(1 + zl, y_down)
-        elif step == 4:
-            from_side(3, 3 - 3 * zl)
-        elif step == 5:
-            from_side(3, 2 - zl)
-        elif step == 6:
-            from_side(3, 3 * zl)
-
-    def during_inner(step):
-        if step == 0:
-            from_side(3, 1 + zl)
+    def own_near(k, onward, passed):
+        arrive(0, k, 0, 2)
+        arrive(0, k, 2, 2)
+        send(0, 0, k, passed, 2, onward)
+        send(0, 0, k, 0, 4, twin)
+
+    def own_far():
+        for half in (0, 2):
+            arrive(0, 2, half, 2)
+        send(0, 0, 2, 0, 4, twin)
+
+    def next_door():
+        for half in (0, 2):
+            arrive(1, 0, half, 2)
+            send(1, 2, 0, half, 2, inner)
+        send(1, 1, 0, kept, 2, up, down)
+        send(1, 1, 0, 0, 4, twin)
+
+    def one_further():
+        for half in (0, 2):
+            arrive(2, 0, half, 2)
+        send(2, 2, 0, kept, 2, up, down)
+        send(2, 2, 0, 0, 4, twin)
+
+    def from_beyond():
+        arrive(3, 0, 2 - 2 * zl, 2)
+        send(3, 3, 0, 2 - 2 * zl, 2, inner)
+
+    def far_whole():
+        arrive(3, 0, 2 * zl, 2)
+        send(3, 3, 0, kept, 2, up, down)
+        send(3, 3, 0, 0, 4, twin)
+
+    def near(band):
+        for k, onward, part, side in ((3, up, 0, y_up), (1, down, 1, y_down)):
+            arrive(band, k, kept, 2)
+            send(band, band, k, kept + part, 1, onward)
+            send(band, band, k, kept, 2, side, twin)
+
+    def far(band):
+        for part, side in ((0, y_up), (1, y_down)):
+            arrive(band, 2, kept + part, 1)
+            send(band, band, 2, kept + part, 1, side)
+        send(band, band, 2, kept, 2, twin)
+
+    def side_near(band):
+        for k in (3, 1):
+            arrive(band, k, other, 2)
+            send(band, band, k, other, 2, twin)
+
+    def side_far(band):
+        for part in range(2):
+            arrive(band, 2, other + part, 1)
+        send(band, band, 2, other, 2, twin)
+
+    def complete(group):
+        for band, k in group:
+            if band == 0 or k == 0:
+                arrive(band, k, 0, 4, 1 - core)
+            else:
+                for half in (0, 2):
+                    arrive(band, k, half, 2, 1 - core)
+
+    groups = (
+        ((0, 0), (0, 3), (0, 1), (1, 0)),
+        ((0, 2), (2, 0), (1, 3), (1, 1)),
+        ((3, 0), (1, 2), (2, 3), (2, 1)),
+        ((3, 3), (3, 1), (2, 2), (3, 2)),
+    )
+    polls = (
+        {1: [from_beyond], 3: [own_far], 4: [one_further, lambda: near(1)], 6: [far_whole]},
+        {
+            0: [lambda: far(1)], 1: [lambda: near(2)], 3: [lambda: side_far(1), lambda: near(3)],
+            5: [lambda: side_near(2)], 6: [lambda: far(2)],
+        },
+        {
+            0: [lambda: far(3)], 1: [lambda: side_near(3)], 3: [lambda: side_far(2)],
+            5: [lambda: side_far(3)],
+        },
+        {},
+    )
+    before_group = ([], [lambda: side_near(1)], [], [])
+
+    next_door()
+    own_near(3, up, 0)
+    own_near(1, down, 2)
 
     scale = (NOPE + ROPE) ** -0.5 * LOG2E
     scores, tops = (scores_0, scores_1), (tops_0, tops_1)
@@ -231,10 +231,9 @@
     def rows_of(step):
         return pl.ds(pl.multiple_of(step * PAIR, PAIR), PAIR)
 
-    def score(band, q, first, slot, top):
-        keys = jnp.concatenate(
-            [bands[band][(first + i) // ROWS] for i in range(0, CHUNK, ROWS)], axis=1
-        )
+    def score(group, q, first, slot, top):
+        band, k = groups[group][first // CHUNK]
+        keys = jnp.concatenate([bands[band][2 * k], bands[band][2 * k + 1]], axis=1)
         s = dot(q, keys)
         scores[slot][:, pl.ds(first, CHUNK)] = s
         for i in range(0, CHUNK, 128):
@@ -242,21 +241,20 @@
             top = part if top is None else jnp.maximum(top, part)
         return top
 
-    def attend(band, step, slot, ahead):
+    def attend(group, step, slot, ahead):
         here = rows_of(step)
         top = jnp.broadcast_to(jnp.max(tops[slot][...], axis=1, keepdims=True), (PAIR, 128)) * scale
-        if band == 0:
-            so_far, sums = jnp.zeros((PAIR, LATENT), F32), jnp.zeros((PAIR, 128), F32)
+        if group == 0:
+            sums = jnp.zeros((PAIR, 128), F32)
         else:
             before = best[here, :]
             top = jnp.maximum(top, before)
             fade = jnp.exp2(before - top)
             sums = total[here, :] * fade
-            so_far = None
         gained, next_top = None, None
         for first in parts:
             if ahead:
-                next_top = score(band, wide_q[rows_of(step + 1), :], first, 1 - slot, next_top)
+                next_top = score(group, wide_q[rows_of(step + 1), :], first, 1 - slot, next_top)
             weights = []
             for i in range(0, CHUNK, 128):
                 w = jnp.exp2(scores[slot][:, pl.ds(first + i, 128)] * scale - top)
@@ -266,9 +264,9 @@
             gained = more if gained is None else gained + more
         if ahead:
             tops[1 - slot][...] = next_top
-        if band > 0:
+        if group > 0:
             gained = gained + context[here, :] * jnp.concatenate([fade] * 4, axis=1)
-        if band < 3:
+        if group < 3:
             best[here, :] = top
             total[here, :] = sums
             context[here, :] = gained
@@ -294,45 +292,46 @@
             device_id=mates[i], device_id_type=MESH,
         )
 
-    for band, between in enumerate((during_own, during_outer, during_inner, None)):
-        if band > 0:
-            complete(band)
-        if band == 3:
+    for group in range(4):
+        for wait in before_group[group]:
+            wait()
+        complete(groups[group])
+        if group == 3:
             loads[2].wait()
 
-        def turn(place, _, band=band):
-            value[pl.ds(pl.multiple_of(place * ROWS, ROWS), ROWS), :] = bands[band][place, :LATENT].T
-            return 0
-
-        lax.fori_loop(0, BAND, turn, 0)
+        for i, (band, k) in enumerate(groups[group]):
+            for c in range(2):
+                taken = bands[band][2 * k + c, :LATENT]
+                value[pl.ds((2 * i + c) * ROWS, ROWS), :] = taken.T
         top = None
         for first in parts:
-            top = score(band, wide_q[rows_of(0), :], first, 0, top)
+            top = score(group, wide_q[rows_of(0), :], first, 0, top)
         tops[0][...] = top
 
-        def go(i, _, band=band, between=between):
+        def go(i, _, group=group):
             for slot in range(2):
-                attend(band, 2 * i + slot, slot, True)
+                attend(group, 2 * i + slot, slot, True)
                 for n in range(slot, STEPS - 2, 2):
-                    if between is not None:
+                    if n in polls[group]:
 
                         @pl.when(i == n // 2)
                         def _(n=n):
-                            between(n)
+                            for wait in polls[group][n]:
+                                wait()
 
             return 0
 
         lax.fori_loop(0, STEPS // 2 - 1, go, 0)
-        attend(band, STEPS - 2, 0, True)
-        if between is not None:
-            between(STEPS - 2)
-        attend(band, STEPS - 1, 1, False)
+        attend(group, STEPS - 2, 0, True)
+        for wait in polls[group].get(STEPS - 2, []):
+            wait()
+        attend(group, STEPS - 1, 1, False)
 
     out[:, pl.ds(pl.multiple_of(head * (HEADS * VHEAD), 128), HEADS * VHEAD)] = attended[
         pl.ds(pl.multiple_of(head * 16, 16), 16), :
     ]
-    for number in range(len(sent)):
-        transfer(0, 0, 0, 0, twin, number, core).wait_send()
+    for number, length in enumerate(sent):
+        transfer(0, 0, 0, 0, length, twin, number, core).wait_send()
 
     def finish(step, _):
         for i in range(7):
@@ -382,8 +381,8 @@
             pltpu.VMEM((HEADS, NOPE, LATENT), BF16),
             pltpu.VMEM((HEADS, LATENT, VHEAD), BF16),
             pltpu.SemaphoreType.DMA((3,)),
-            pltpu.SemaphoreType.DMA((64,)),
-            pltpu.SemaphoreType.DMA((4, BAND, 2)),
+            pltpu.SemaphoreType.DMA((72,)),
+            pltpu.SemaphoreType.DMA((4, BAND, 4)),
             pltpu.SemaphoreType.DMA((STEPS, 7)),
             pltpu.SemaphoreType.DMA((STEPS, 7)),
         ],

time: 65.7 us -> 61.8 us (0.941)
  Pallas kernels: 63.7 us -> 59.8 us
    pallas_call x1, Pallas kernels: 63.7 us -> 59.8 us  [shards(): pl.pallas_call(kernel, out_shape=jax.ShapeDtypeStruct((16, 8 * HEADS * VH...]
where the time goes in v4:
time: 61.8 us; the launch traced here: 61.7 us
  Pallas kernels  59.8 us (97%)
  local copies, waits for them, and re-layouts  1.87 us (3%)
    pallas_call x1, Pallas kernels, shards(): pl.pallas_call(kernel, out_shape=jax.ShapeDtypeStruct((16, 8 * HEADS * VH...  59.8 us
    unnamed x1, local copies, waits for them, and re-layouts  1.87 us

profile of v4, /device:TPU:1, one launch (start us, length us, event | category | flops | bytes accessed | tf_op | source)
XLA Modules:
  0.0 61.7 jit_solution(4142757084391536477)
XLA Ops:
  0.0 59.8 %shard_map.64 = bf16[16,16384]{1,0:T(8,128)(2,1)} custom-call(s32[32]{0:T(128)} %order.1, s32[4096]{0:T(1024)} %segment.1, bf16[576,128]{1,0:T(8,128)(2,1)} %bitcast.1, bf16[128,3072]{1,0:T(8,128)(2,1)} %queries_hbm.1, bf16[16,128,512]{2,1,0:T(8,128)(2,1)} %w_key_hbm.1, bf16[16,512,128]{2,1,0:T(8,128)(2,1)} %w_value_hbm.1), custom_call_target="tpu_custom_call" | custom-call | flops 20000000000 | bytes 6291456 | tf_op jit(solution)/shard_map/pallas_call | solution.py:353
  59.8 1.9 %copy.8 = bf16[16,16384]{1,0:T(8,128)(2,1)} copy(bf16[16,16384]{1,0:T(8,128)(2,1)} %shard_map.64) | data formatting | bytes 1048576

commit v5 on v4

--- a/solution.py
+++ b/solution.py
@@ -89,6 +89,13 @@
             transfer(band, landing, k, first, length, device, len(sent), core).start()
             sent.append(length)
 
+    drained = []
+
+    def drain(until):
+        for number in range(len(drained), until):
+            transfer(0, 0, 0, 0, sent[number], twin, number, core).wait_send()
+            drained.append(number)
+
     def arrive(band, k, first, length, core_of=core):
         transfer(band, band, k, first, length, twin, 0, core_of).wait_recv()
 
@@ -207,15 +214,13 @@
         ((3, 3), (3, 1), (2, 2), (3, 2)),
     )
     polls = (
-        {1: [from_beyond], 3: [own_far], 4: [one_further, lambda: near(1)], 6: [far_whole]},
+        {0: [from_beyond], 2: [lambda: near(1)], 3: [own_far], 4: [one_further], 5: [far_whole], 6: [lambda: far(1)]},
         {
-            0: [lambda: far(1)], 1: [lambda: near(2)], 3: [lambda: side_far(1), lambda: near(3)],
-            5: [lambda: side_near(2)], 6: [lambda: far(2)],
+            0: [lambda: near(2)], 1: [lambda: side_far(1), lambda: near(3)],
+            3: [lambda: far(2)], 4: [lambda: side_near(2), lambda: far(3)],
+            5: [lambda: side_near(3)], 6: [lambda: side_far(2)],
         },
-        {
-            0: [lambda: far(3)], 1: [lambda: side_near(3)], 3: [lambda: side_far(2)],
-            5: [lambda: side_far(3)],
-        },
+        {1: [lambda: side_far(3)]},
         {},
     )
     before_group = ([], [lambda: side_near(1)], [], [])
@@ -288,7 +293,7 @@
         return pltpu.make_async_remote_copy(
             src_ref=attended.at[pl.ds(pl.multiple_of(mate * 16, 16), 16), columns_of(0, step)],
             dst_ref=out.at[:, columns_of(head, step)],
-            send_sem=out_send.at[step, i], recv_sem=out_recv.at[step, i],
+            send_sem=out_send.at[i], recv_sem=out_recv.at[i],
             device_id=mates[i], device_id_type=MESH,
         )
 
@@ -330,22 +335,17 @@
     out[:, pl.ds(pl.multiple_of(head * (HEADS * VHEAD), 128), HEADS * VHEAD)] = attended[
         pl.ds(pl.multiple_of(head * 16, 16), 16), :
     ]
-    for number, length in enumerate(sent):
-        transfer(0, 0, 0, 0, length, twin, number, core).wait_send()
-
-    def finish(step, _):
-        for i in range(7):
-            deliver(step, i).wait_send()
-            sender = (head + 7 - i) % 8
-            pltpu.make_async_remote_copy(
-                src_ref=attended.at[pl.ds(0, 16), columns_of(0, step)],
-                dst_ref=out.at[:, columns_of(sender, step)],
-                send_sem=out_send.at[step, i], recv_sem=out_recv.at[step, i],
-                device_id=mates[i], device_id_type=MESH,
-            ).wait_recv()
-        return 0
-
-    lax.fori_loop(0, STEPS, finish, 0)
+    drain(len(sent))
+    for i in range(7):
+        mate, sender = mates[i][1], (head + 7 - i) % 8
+        whole = pltpu.make_async_remote_copy(
+            src_ref=attended.at[pl.ds(pl.multiple_of(mate * 16, 16), 16), :],
+            dst_ref=out.at[:, pl.ds(pl.multiple_of(sender * (HEADS * VHEAD), 128), HEADS * VHEAD)],
+            send_sem=out_send.at[i], recv_sem=out_recv.at[i],
+            device_id=mates[i], device_id_type=MESH,
+        )
+        whole.wait_send()
+        whole.wait_recv()
 
 
 def shards(queries, latent_keys, w_key_up, w_value_up, slab_order, segment_ids):
@@ -383,8 +383,8 @@
             pltpu.SemaphoreType.DMA((3,)),
             pltpu.SemaphoreType.DMA((72,)),
             pltpu.SemaphoreType.DMA((4, BAND, 4)),
-            pltpu.SemaphoreType.DMA((STEPS, 7)),
-            pltpu.SemaphoreType.DMA((STEPS, 7)),
+            pltpu.SemaphoreType.DMA((7,)),
+            pltpu.SemaphoreType.DMA((7,)),
         ],
         compiler_params=pltpu.CompilerParams(
             collective_id=0, has_side_effects=True, vmem_limit_bytes=56 * 2**20

time: 61.8 us -> 59.3 us (0.960)
  Pallas kernels: 59.8 us -> 57.3 us
    pallas_call x1, Pallas kernels: 59.8 us -> 57.3 us  [shards(): pl.pallas_call(kernel, out_shape=jax.ShapeDtypeStruct((16, 8 * HEADS * VH...]
where the time goes in v5:
time: 59.3 us; the launch traced here: 59.2 us
  Pallas kernels  57.3 us (97%)
  local copies, waits for them, and re-layouts  1.87 us (3%)
    pallas_call x1, Pallas kernels, shards(): pl.pallas_call(kernel, out_shape=jax.ShapeDtypeStruct((16, 8 * HEADS * VH...  57.3 us
    unnamed x1, local copies, waits for them, and re-layouts  1.87 us

profile of v5, /device:TPU:1, one launch (start us, length us, event | category | flops | bytes accessed | tf_op | source)
XLA Modules:
  0.0 59.2 jit_solution(831634172569480262)
XLA Ops:
  0.0 57.3 %shard_map.64 = bf16[16,16384]{1,0:T(8,128)(2,1)} custom-call(s32[32]{0:T(128)} %order.1, s32[4096]{0:T(1024)} %segment.1, bf16[576,128]{1,0:T(8,128)(2,1)} %bitcast.1, bf16[128,3072]{1,0:T(8,128)(2,1)} %queries_hbm.1, bf16[16,128,512]{2,1,0:T(8,128)(2,1)} %w_key_hbm.1, bf16[16,512,128]{2,1,0:T(8,128)(2,1)} %w_value_hbm.1), custom_call_target="tpu_custom_call" | custom-call | flops 20000000000 | bytes 6291456 | tf_op jit(solution)/shard_map/pallas_call | solution.py:353
  57.3 1.9 %copy.8 = bf16[16,16384]{1,0:T(8,128)(2,1)} copy(bf16[16,16384]{1,0:T(8,128)(2,1)} %shard_map.64) | data formatting | bytes 1048576

commit v6 on v5

--- a/solution.py
+++ b/solution.py
@@ -102,6 +102,7 @@
     kept, other = 2 * (y % 2), 2 - 2 * (y % 2)
     for half in (0, 2):
         send(0, 0, 0, half, 2, up, down)
+    for half in (kept, other):
         send(0, 1, 0, half, 2, outer)
     send(0, 3, 0, 2 * zl, 2, beyond)
     send(0, 0, 0, 0, 4, twin)
@@ -156,16 +157,17 @@
         send(0, 0, 2, 0, 4, twin)
 
     def next_door():
-        for half in (0, 2):
-            arrive(1, 0, half, 2)
-            send(1, 2, 0, half, 2, inner)
+        arrive(1, 0, kept, 2)
         send(1, 1, 0, kept, 2, up, down)
+        send(1, 2, 0, kept, 2, inner)
+        arrive(1, 0, other, 2)
+        send(1, 2, 0, other, 2, inner)
         send(1, 1, 0, 0, 4, twin)
 
     def one_further():
-        for half in (0, 2):
-            arrive(2, 0, half, 2)
+        arrive(2, 0, kept, 2)
         send(2, 2, 0, kept, 2, up, down)
+        arrive(2, 0, other, 2)
         send(2, 2, 0, 0, 4, twin)
 
     def from_beyond():

time: 59.3 us -> 59.3 us (level)
  no operation moved by 1% of the time
where the time goes in v6:
time: 59.3 us; the launch traced here: 59.2 us
  Pallas kernels  57.3 us (97%)
  local copies, waits for them, and re-layouts  1.87 us (3%)
    pallas_call x1, Pallas kernels, shards(): pl.pallas_call(kernel, out_shape=jax.ShapeDtypeStruct((16, 8 * HEADS * VH...  57.3 us
    unnamed x1, local copies, waits for them, and re-layouts  1.87 us

profile of v6, /device:TPU:1, one launch (start us, length us, event | category | flops | bytes accessed | tf_op | source)
XLA Modules:
  0.0 59.2 jit_solution(9272866734790830872)
XLA Ops:
  0.0 57.3 %shard_map.64 = bf16[16,16384]{1,0:T(8,128)(2,1)} custom-call(s32[32]{0:T(128)} %order.1, s32[4096]{0:T(1024)} %segment.1, bf16[576,128]{1,0:T(8,128)(2,1)} %bitcast.1, bf16[128,3072]{1,0:T(8,128)(2,1)} %queries_hbm.1, bf16[16,128,512]{2,1,0:T(8,128)(2,1)} %w_key_hbm.1, bf16[16,512,128]{2,1,0:T(8,128)(2,1)} %w_value_hbm.1), custom_call_target="tpu_custom_call" | custom-call | flops 20000000000 | bytes 6291456 | tf_op jit(solution)/shard_map/pallas_call | solution.py:355
  57.3 1.9 %copy.8 = bf16[16,16384]{1,0:T(8,128)(2,1)} copy(bf16[16,16384]{1,0:T(8,128)(2,1)} %shard_map.64) | data formatting | bytes 1048576

commit v7 on v6

--- a/solution.py
+++ b/solution.py
@@ -216,16 +216,18 @@
         ((3, 3), (3, 1), (2, 2), (3, 2)),
     )
     polls = (
-        {0: [from_beyond], 2: [lambda: near(1)], 3: [own_far], 4: [one_further], 5: [far_whole], 6: [lambda: far(1)]},
+        {1: [from_beyond], 3: [lambda: near(1)], 5: [one_further, own_far]},
         {
-            0: [lambda: near(2)], 1: [lambda: side_far(1), lambda: near(3)],
-            3: [lambda: far(2)], 4: [lambda: side_near(2), lambda: far(3)],
-            5: [lambda: side_near(3)], 6: [lambda: side_far(2)],
+            0: [lambda: near(2)], 2: [lambda: side_far(1), lambda: near(3)],
+            5: [lambda: far(2)], 6: [lambda: side_near(2)],
         },
-        {1: [lambda: side_far(3)]},
+        {
+            0: [lambda: far(3), lambda: side_near(3)], 1: [lambda: side_far(2)],
+            5: [lambda: side_far(3)],
+        },
         {},
     )
-    before_group = ([], [lambda: side_near(1)], [], [])
+    before_group = ([], [far_whole, lambda: far(1), lambda: side_near(1)], [], [])
 
     next_door()
     own_near(3, up, 0)

time: 59.3 us -> 59.8 us (level)
  no operation moved by 1% of the time
where the time goes in v7:
time: 59.8 us; the launch traced here: 59.7 us
  Pallas kernels  57.8 us (97%)
  local copies, waits for them, and re-layouts  1.87 us (3%)
    pallas_call x1, Pallas kernels, shards(): pl.pallas_call(kernel, out_shape=jax.ShapeDtypeStruct((16, 8 * HEADS * VH...  57.8 us
    unnamed x1, local copies, waits for them, and re-layouts  1.87 us

profile of v7, /device:TPU:1, one launch (start us, length us, event | category | flops | bytes accessed | tf_op | source)
XLA Modules:
  0.0 59.7 jit_solution(14597588751938858619)
XLA Ops:
  0.0 57.8 %shard_map.64 = bf16[16,16384]{1,0:T(8,128)(2,1)} custom-call(s32[32]{0:T(128)} %order.1, s32[4096]{0:T(1024)} %segment.1, bf16[576,128]{1,0:T(8,128)(2,1)} %bitcast.1, bf16[128,3072]{1,0:T(8,128)(2,1)} %queries_hbm.1, bf16[16,128,512]{2,1,0:T(8,128)(2,1)} %w_key_hbm.1, bf16[16,512,128]{2,1,0:T(8,128)(2,1)} %w_value_hbm.1), custom_call_target="tpu_custom_call" | custom-call | flops 20000000000 | bytes 6291456 | tf_op jit(solution)/shard_map/pallas_call | solution.py:357
  57.8 1.9 %copy.8 = bf16[16,16384]{1,0:T(8,128)(2,1)} copy(bf16[16,16384]{1,0:T(8,128)(2,1)} %shard_map.64) | data formatting | bytes 1048576
